TPU v7x, 256 devices: a whole 4x4x8 slice. The times are simulated.
256 devices in a mesh: pop: 8 (over y, core), mp: 32 (over x, z).
Axes of the slice: x: 4, y: 4, z: 8, core: 2. Of those that a mesh axis runs over, the one named last changes fastest.
Arguments:
- tokens: bfloat16 [4096, 4096], P('pop', 'mp'), may hold values from -6 to 6
- norm_gain: float32 [4096], replicated, may hold values from 0.25 to 1.75
- gate_weight: bfloat16 [4096, 14848], P(None, 'mp'), may hold values from -0.09375 to 0.09375
- up_weight: bfloat16 [4096, 14848], P(None, 'mp'), may hold values from -0.09375 to 0.09375
- down_weight: bfloat16 [14848, 4096], P('mp'), may hold values from -0.09375 to 0.09375
- gate_left: bfloat16 [32, 4, 4096], P('pop'), may hold values from -4 to 4
- up_left: bfloat16 [32, 4, 4096], P('pop'), may hold values from -4 to 4
- down_right: bfloat16 [32, 4, 4096], P('pop'), may hold values from -4 to 4
- gate_right: bfloat16 [32, 4, 14848], P('pop', None, 'mp'), may hold values from -4 to 4
- up_right: bfloat16 [32, 4, 14848], P('pop', None, 'mp'), may hold values from -4 to 4
- down_left: bfloat16 [32, 4, 14848], P('pop', None, 'mp'), may hold values from -4 to 4
- fitness: float32 [64], P('pop'), may hold values from -15 to 15
Outputs:
- mixed: bfloat16 [4096, 4096], P('pop', 'mp')
- gate_step: bfloat16 [4096, 14848], P('pop', 'mp')
- up_step: bfloat16 [4096, 14848], P('pop', 'mp')
- down_step: bfloat16 [14848, 4096], P('mp', 'pop')
All inputs are finite; a program needn't handle non-finite values.
Results may differ from a plain program's by a relative error of at most 0.02.
Values may be sent and summed in bfloat16 or wider, within the bound.
A program may use at most 128 MiB of HBM per device.

v0:
```python
import math

import jax
import jax.numpy as jnp
from jax import lax
from jax.sharding import PartitionSpec as P

FF = 14848


def row_weighting(rows, pairs, rank, rows_member):
    member = jnp.arange(rows, dtype=jnp.int32) // rows_member
    column_pair = jnp.arange(pairs * rank, dtype=jnp.int32) // rank
    polarity = (1 - 2 * (member % 2)).astype(jnp.float32)
    return jnp.where(
        (member // 2)[:, None] == column_pair[None, :], polarity[:, None], jnp.float32(0.0)
    )


def project_rank(inputs, left):
    flat_left = left.reshape(-1, left.shape[2])
    return lax.dot_general(
        inputs, flat_left, (((1,), (1,)), ((), ())), preferred_element_type=jnp.float32
    )


def perturbed(inputs, weight, left, right, weighting, spread):
    projected = project_rank(inputs, left)
    base = jnp.dot(inputs, weight, preferred_element_type=jnp.float32)
    flat_right = right.reshape(-1, right.shape[2]).astype(jnp.float32)
    return base + jnp.dot(
        weighting * projected * spread, flat_right, precision=lax.Precision.HIGHEST
    )


def outer_sum(left, right, pair_weight):
    scaled = (left.astype(jnp.float32) * pair_weight[:, None, None]).reshape(-1, left.shape[2])
    flat_right = right.astype(jnp.float32).reshape(-1, right.shape[2])
    return lax.dot_general(
        scaled, flat_right, (((0,), (0,)), ((), ())), precision=lax.Precision.HIGHEST
    )


def total_down(partial_value, feature_block):
    full_sum = lax.psum(partial_value, "mp").astype(jnp.float32)
    summed = lax.dynamic_slice_in_dim(
        full_sum, lax.axis_index("mp") * feature_block, feature_block, 1
    )
    return summed


def per_device(
    tokens,
    norm_gain,
    gate_weight,
    up_weight,
    down_weight,
    gate_left,
    up_left,
    down_right,
    gate_right,
    up_right,
    down_left,
    fitness,
):
    rows_dev = tokens.shape[0]
    feature_block = tokens.shape[1]
    pairs_dev = gate_left.shape[0]
    rank = gate_left.shape[1]
    model_width = gate_left.shape[2]
    rows_member = rows_dev // (2 * pairs_dev)
    weighting = row_weighting(rows_dev, pairs_dev, rank, rows_member)
    whole = lax.all_gather(tokens, "mp", axis=1, tiled=True)
    widened = whole.astype(jnp.float32)
    row_scale = lax.rsqrt(jnp.mean(widened * widened, axis=1, keepdims=True) + 1e-06)
    normed = (widened * row_scale * norm_gain[None, :]).astype(jnp.bfloat16)
    spread_in = 0.5 / math.sqrt(model_width)
    gate = perturbed(normed, gate_weight, gate_left, gate_right, weighting, spread_in)
    up_value = perturbed(normed, up_weight, up_left, up_right, weighting, spread_in)
    hidden = (jax.nn.silu(gate) * up_value).astype(jnp.bfloat16)
    spread_hidden = 0.5 / math.sqrt(FF)
    partial_value = perturbed(
        hidden, down_weight, down_left, down_right, weighting, spread_hidden
    ).astype(jnp.bfloat16)
    down_block = total_down(partial_value, feature_block)
    mixed = (tokens.astype(jnp.float32) + down_block).astype(jnp.bfloat16)
    all_fitness = lax.all_gather(fitness, "pop", axis=0, tiled=True)
    pairs_total = all_fitness.shape[0] // 2
    center = jnp.mean(all_fitness)
    spread_sq = jnp.mean((all_fitness - center) * (all_fitness - center))
    shaped = (all_fitness - center) * lax.rsqrt(spread_sq + 1e-05)
    pair_weight = (shaped[0::2] - shaped[1::2]) / math.sqrt(pairs_total * rank)
    pop_count = lax.axis_size("pop")
    row_block = model_width // pop_count
    gate_full, up_full, down_full = (
        lax.all_gather(gate_left, "pop", axis=0, tiled=True),
        lax.all_gather(up_left, "pop", axis=0, tiled=True),
        lax.all_gather(down_right, "pop", axis=0, tiled=True),
    )
    offset = lax.axis_index("pop") * row_block
    gate_lefts = lax.dynamic_slice_in_dim(gate_full, offset, row_block, 2)
    up_lefts = lax.dynamic_slice_in_dim(up_full, offset, row_block, 2)
    down_rights = lax.dynamic_slice_in_dim(down_full, offset, row_block, 2)
    gate_rights, up_rights, down_lefts = (
        lax.all_gather(gate_right, "pop", axis=0, tiled=True),
        lax.all_gather(up_right, "pop", axis=0, tiled=True),
        lax.all_gather(down_left, "pop", axis=0, tiled=True),
    )
    gate_step = outer_sum(gate_lefts, gate_rights, pair_weight).astype(jnp.bfloat16)
    up_step = outer_sum(up_lefts, up_rights, pair_weight).astype(jnp.bfloat16)
    down_step = outer_sum(down_lefts, down_rights, pair_weight).astype(jnp.bfloat16)
    return (mixed, gate_step, up_step, down_step)


def solution(mesh):
    in_specs = (
        P("pop", "mp"),
        P(),
        P(None, "mp"),
        P(None, "mp"),
        P("mp", None),
        P("pop", None, None),
        P("pop", None, None),
        P("pop", None, None),
        P("pop", None, "mp"),
        P("pop", None, "mp"),
        P("pop", None, "mp"),
        P("pop"),
    )
    out_specs = (P("pop", "mp"), P("pop", "mp"), P("pop", "mp"), P("mp", "pop"))
    return jax.shard_map(
        per_device, mesh=mesh, in_specs=in_specs, out_specs=out_specs, check_vma=False
    )
```

profile of v0, /device:TPU:8, one launch (start us, length us, event | category | flops | bytes accessed | tf_op | source)
XLA Modules:
  0.0 355.8 jit_solution(8209392825316174083)
XLA Ops:
  7.2 0.7 all-gather.5.cloned.1.call-update
  7.9 0.0 all-gather.7.cloned.1.call-start
  8.0 0.7 all-gather.7.cloned.1.call-update
  8.7 0.0 all-gather.9.cloned.1.call-start
  8.7 0.7 all-gather.9.cloned.1.call-update
  9.4 0.5 all-gather.11.cloned.1.call-update
  10.0 0.0 all-reduce.3.cloned.1.call-start
  10.0 0.9 reshape.99
  11.0 0.9 reshape.101
  11.9 0.9 reshape.104
  12.9 0.7 reshape.100
  13.6 0.7 reshape.102
  14.3 0.7 reshape.103
  15.1 81.4 %all-gather.5.cloned.1.call-done = bf16[512,4096]{1,0:T(8,128)(2,1)} async-done(((bf16[512,128]{1,0:T(8,128)(2,1)}), bf16[512,4096]{1,0:T(8,128)(2,1)}) %all-gather.5.cloned.1.call-update) | async-done | bytes 4194320 | tf_op jit(solution)/shard_map/all_gather | solution.py:73
  96.5 3.2 fusion
  99.8 0.2 copy-done
  100.0 1.7 fusion.2
  101.6 0.4 copy-done.7
  102.0 2.3 fusion.36
  104.4 1.2 fusion.10
  105.6 1.2 fusion.9
  106.8 2.3 fusion.37
  109.1 0.6 convolution_add_fusion.1
  109.7 0.8 fusion.7
  110.5 0.2 fusion.8
  110.7 0.6 copy-done.1
  111.3 2.4 fusion.38
  113.7 5.9 %add_convert_fusion = bf16[512,4096]{1,0:T(8,128)(2,1)} fusion(f32[512,4096]{1,0:T(8,128)S(1)} %fusion.38, f32[512,16]{0,1:T(8,128)S(1)} %fusion.8, bf16[16,4096]{1,0:T(8,128)(2,1)S(1)} %reshape.104), kind=kOutput, calls=%fused_computation.5 | convolution fusion | flops 406847488 | bytes 12746752 | tf_op jit(solution)/shard_map/dot_general | solution.py:31
  119.7 0.6 copy-done.10
  120.3 0.6 dynamic-slice
  121.6 0.2 dynamic-update-slice
  121.8 10.0 %all-reduce = f32[64]{0:T(128)S(1)} all-reduce(f32[64]{0:T(128)S(1)} %dynamic-update-slice), channel_id=1, replica_groups=mesh['pop'=8,'mp'=32] {'pop'}, use_global_device_ids=true, to_apply=%add | all-reduce | flops 64 | bytes 512
  131.8 0.6 reduce_sum.28
  133.0 0.6 multiply_reduce_fusion
  134.4 0.1 slice.6
  134.5 0.1 slice.7
  134.6 12.8 %all_gather.27 = bf16[32,4,464]{2,1,0:T(4,128)(2,1)S(1)} all-gather(bf16[4,4,464]{2,1,0:T(4,128)(2,1)S(1)} %copy-done.3), channel_id=1, replica_groups=mesh['pop'=8,'mp'=32] {'pop'}, dimensions={0}, use_global_device_ids=true | all-gather | bytes 133632 | tf_op jit(solution)/shard_map/all_gather | solution.py:105
  147.4 12.8 %all_gather.29 = bf16[32,4,464]{2,1,0:T(4,128)(2,1)S(1)} all-gather(bf16[4,4,464]{2,1,0:T(4,128)(2,1)S(1)} %copy-done.4), channel_id=1, replica_groups=mesh['pop'=8,'mp'=32] {'pop'}, dimensions={0}, use_global_device_ids=true | all-gather | bytes 133632 | tf_op jit(solution)/shard_map/all_gather | solution.py:106
  160.2 12.7 %all_gather.30 = bf16[32,4,464]{2,1,0:T(4,128)(2,1)S(1)} all-gather(bf16[4,4,464]{2,1,0:T(4,128)(2,1)S(1)} %copy-done.5), channel_id=1, replica_groups=mesh['pop'=8,'mp'=32] {'pop'}, dimensions={0}, use_global_device_ids=true | all-gather | bytes 133632 | tf_op jit(solution)/shard_map/all_gather | solution.py:107
  172.9 1.0 constant_dynamic-slice_fusion.2
  173.9 1.0 constant_dynamic-slice_fusion.1
  174.8 3.8 %all-gather.11.cloned.1.call-done = bf16[32,4,4096]{2,1,0:T(4,128)(2,1)} async-done(((bf16[4,4,4096]{2,1,0:T(4,128)(2,1)}), bf16[32,4,4096]{2,1,0:T(4,128)(2,1)}) %all-gather.11.cloned.1.call-update) | async-done | bytes 1048592 | tf_op jit(solution)/shard_map/all_gather | solution.py:98
  178.7 0.9 constant_dynamic-slice_fusion
  179.6 1.4 fusion.4
  181.0 1.4 fusion.5
  182.4 1.4 fusion.6
  183.9 163.8 %all-reduce.3.cloned.1.call-done = bf16[512,4096]{1,0:T(8,128)(2,1)} async-done(((bf16[512,4096]{1,0:T(8,128)(2,1)}), bf16[512,4096]{1,0:T(8,128)(2,1)}) %all-reduce.3.cloned.1.call-update) | async-done | bytes 4194320 | tf_op jit(solution)/shard_map/psum | solution.py:45
  347.7 1.6 add_convert_fusion.1
  (29 shorter events, 0.2 us)
Async XLA Ops:
  7.2 92.6 %copy-start.6 = (f32[4096]{0:T(1024)S(1)}, f32[4096]{0:T(1024)}, u32[]{:S(2)}) copy-start(f32[4096]{0:T(1024)} %param.13) | copy-start | bytes 49156
  7.2 89.3 %all-gather.5.cloned.1.call-start = ((), (), s32[]{:S(2)}) async-start(), calls=%async_computation | async-start | bytes 4325376 | tf_op jit(solution)/shard_map/all_gather | solution.py:73
  7.9 165.0 %all-gather.7.cloned.1.call-start = ((), (), s32[]{:S(2)}) async-start(), calls=%async_computation.2 | async-start | bytes 1179648 | tf_op jit(solution)/shard_map/all_gather | solution.py:96
  8.7 165.2 %all-gather.9.cloned.1.call-start = ((), (), s32[]{:S(2)}) async-start(), calls=%async_computation.3 | async-start | bytes 1179648 | tf_op jit(solution)/shard_map/all_gather | solution.py:97
  9.4 169.3 %all-gather.11.cloned.1.call-start = ((), (), s32[]{:S(2)}) async-start(), calls=%async_computation.4 | async-start | bytes 1179648 | tf_op jit(solution)/shard_map/all_gather | solution.py:98
  10.0 337.7 %all-reduce.3.cloned.1.call-start = ((), (), s32[]{:S(2)}) async-start(), calls=%async_computation.1 | async-start | bytes 8388608 | tf_op jit(solution)/shard_map/psum | solution.py:45
  96.5 3.4 copy-start
  100.0 2.1 copy-start.7
  104.4 2.4 copy-start.8
  109.1 2.2 copy-start.1
  119.6 0.7 copy-start.10
  119.6 1.9 copy-start.9
  119.6 15.0 %copy-start.3 = (bf16[4,4,464]{2,1,0:T(4,128)(2,1)S(1)}, bf16[4,4,464]{2,1,0:T(4,128)(2,1)}, u32[]{:S(2)}) copy-start(bf16[4,4,464]{2,1,0:T(4,128)(2,1)} %param.20) | copy-start | bytes 44548
  119.6 27.8 %copy-start.4 = (bf16[4,4,464]{2,1,0:T(4,128)(2,1)S(1)}, bf16[4,4,464]{2,1,0:T(4,128)(2,1)}, u32[]{:S(2)}) copy-start(bf16[4,4,464]{2,1,0:T(4,128)(2,1)} %param.21) | copy-start | bytes 44548
  119.6 40.5 %copy-start.5 = (bf16[4,4,464]{2,1,0:T(4,128)(2,1)S(1)}, bf16[4,4,464]{2,1,0:T(4,128)(2,1)}, u32[]{:S(2)}) copy-start(bf16[4,4,464]{2,1,0:T(4,128)(2,1)} %param.22) | copy-start | bytes 44548
  119.7 228.0 %copy-start.2 = (bf16[512,128]{1,0:T(8,128)(2,1)S(1)}, bf16[512,128]{1,0:T(8,128)(2,1)}, u32[]{:S(2)}) copy-start(bf16[512,128]{1,0:T(8,128)(2,1)} %param.12) | copy-start | bytes 393220
Sparse Core Ops, SparseCore 0:
  10.5 85.9 all-gather.4
  98.4 24.4 all-gather.6
  124.8 25.8 all-gather.8
  152.4 26.2 all-gather.10
  182.1 165.5 all-reduce.2
where the time goes:
time: 356 us
  waiting for transfers between devices  252 us (71%)
  blocking collectives  48.3 us (14%)
  matrix products  21.2 us (6%)
  between operations  16 us (4%)
  local copies, waits for them, and re-layouts  10.8 us (3%)
  other arithmetic  7.72 us (2%)
    psum x1, waiting for transfers between devices, total_down(): full_sum = lax.psum(partial_value, 'mp').astype(jnp.float32)  164 us
    all_gather x1, waiting for transfers between devices, per_device(): whole = lax.all_gather(tokens, 'mp', axis=1, tiled=True)  81.4 us
    all_gather x1, blocking collectives, per_device(): lax.all_gather(gate_right, 'pop', axis=0, tiled=True)  12.8 us
    all_gather x1, blocking collectives, per_device(): lax.all_gather(up_right, 'pop', axis=0, tiled=True)  12.8 us
    all_gather x1, blocking collectives, per_device(): lax.all_gather(down_left, 'pop', axis=0, tiled=True)  12.7 us
    unnamed x1, blocking collectives  9.99 us
    dot_general x3, matrix products, perturbed(): jnp.dot(weighting * projected * spread, flat_right, precision=lax.Precisi...  7.27 us
  transfers between devices with their start and end apart: 5, of which 3 were waited for; matrix products, arithmetic and copies ran while one was open for 10% of the time, Pallas kernels for 0%

commit v1 on v0

v1 whole, which is shorter than its diff:
```python
import math

import jax
import jax.numpy as jnp
from jax import lax
from jax.experimental import pallas as pl
from jax.experimental.pallas import tpu as pltpu
from jax.sharding import PartitionSpec as P

MESH = pl.DeviceIdType.MESH
BF = jnp.bfloat16
F32 = jnp.float32

NX, NZ, NPOP = 4, 8, 8
ROWS, FB, FFB, D, FF = 512, 128, 464, 4096, 14848
NCH = 4
RC = ROWS // NCH
SLOTS = 8
OWN = 31

TREE = (
    (((0, 0), (1, 0)), ((0, 0), (3, 0)), ((0, 0), (0, 1)), ((0, 0), (0, 7))),
    (((1, 0), (2, 0)), ((0, 7), (3, 7)), ((1, 0), (1, 1)), ((0, 7), (0, 6))),
    (((0, 7), (1, 7)), ((0, 1), (3, 1)), ((0, 1), (0, 2)), ((0, 6), (0, 5))),
    (((0, 6), (1, 6)), ((0, 6), (3, 6)), ((2, 0), (2, 1)), ((0, 5), (0, 4))),
    (((0, 5), (1, 5)), ((0, 2), (3, 2)), ((1, 1), (1, 2)), ((2, 0), (2, 7))),
    (((0, 4), (1, 4)), ((3, 6), (2, 6)), ((2, 1), (2, 2)), ((0, 4), (0, 3))),
    (((1, 5), (2, 5)), ((0, 4), (3, 4)), ((1, 2), (1, 3)), ((3, 6), (3, 5))),
    (((1, 4), (2, 4)), ((0, 3), (3, 3)), ((2, 2), (2, 3))),
)
EDGES = [(s, k) + e for s, slot in enumerate(TREE) for k, e in enumerate(slot)]
OFFSET = [e[3] for e in EDGES] + [(0, 0)]
INDEX = {o: n for n, o in enumerate(OFFSET)}
PARENT = [INDEX[e[2]] for e in EDGES]
CHILDREN = [[c for c in range(31) if PARENT[c] == n] for n in range(32)]
GROUP = [list(range(4 * s, 4 * s + 4)) for s in range(SLOTS)]


def slot_of(n):
    return -1 if n == OWN else n // 4


def nt(a, b):
    return lax.dot_general(a, b, (((1,), (1,)), ((), ())), preferred_element_type=F32)


def mm(a, b):
    return jnp.dot(a, b, preferred_element_type=F32)


def kernel(
    tok_h, gain_h, wg_h, wu_h, wd_h, gl_h, ul_h, dr_h, gr_h, ur_h, dl_h, fit_h,
    mixed_ref, gs_h, us_h, ds_h,
    tok, wg, wu, wd, accg, accu, accp, sq, hid, part, rsr,
    gl, ul, dr, gr, ur, dl, lf, rf, lx, rxg, rxu, dlx,
    lsend, rsend, fsend, lrecv, rrecv, frecv, gain, gainp, fit, wcol, gsb, usb, dsb,
    wsem, lsem, osem, ag_send, ag_recv, rs_send, rs_recv, x_send, x_recv,
):
    p = lax.axis_index("pop")
    m = lax.axis_index("mp")
    x, z = m // NZ, m % NZ

    def near(k):
        if k < 2:
            return (p, ((x + (1, NX - 1)[k]) % NX) * NZ + z)
        return (p, x * NZ + (z + (1, NZ - 1)[k - 2]) % NZ)

    def source(n):
        dx, dz = OFFSET[n]
        return ((x + NX - dx) % NX) * NZ + (z + NZ - dz) % NZ

    def peer(j):
        return ((p + j) % NPOP, m)

    own = pltpu.make_async_copy(tok_h, tok.at[OWN], lsem.at[0])
    own.start()
    small = [
        pltpu.make_async_copy(a, b, lsem.at[1 + i])
        for i, (a, b) in enumerate(
            ((gl_h, gl), (ul_h, ul), (dr_h, dr), (gr_h, gr), (ur_h, ur), (dl_h, dl), (gain_h, gain), (fit_h, fit))
        )
    ]
    for c in small:
        c.start()

    bar = pltpu.get_barrier_semaphore()
    for k in range(4):
        pl.semaphore_signal(bar, inc=1, device_id=near(k), device_id_type=MESH)
    for j in range(1, NPOP):
        pl.semaphore_signal(bar, inc=1, device_id=peer(j), device_id_type=MESH)

    for s in range(SLOTS):
        for n in GROUP[s]:
            rows = pl.ds(pl.multiple_of(source(n) * FB, FB), FB)
            pltpu.make_async_copy(wg_h.at[rows], wg.at[pl.ds(n * FB, FB)], wsem.at[s]).start()
            pltpu.make_async_copy(wu_h.at[rows], wu.at[pl.ds(n * FB, FB)], wsem.at[8 + s]).start()
    for s in reversed(range(SLOTS)):
        for n in GROUP[s]:
            cols = pl.ds(pl.multiple_of(source(n) * FB, FB), FB)
            pltpu.make_async_copy(
                wd_h.at[:, cols], wd.at[pl.ds(0, FFB), pl.ds(n * FB, FB)], wsem.at[16 + s]
            ).start()

    def wait_in(s):
        rows = pl.ds(s * 512, 512)
        pltpu.make_async_copy(wg_h.at[pl.ds(0, 512)], wg.at[rows], wsem.at[s]).wait()
        pltpu.make_async_copy(wu_h.at[pl.ds(0, 512)], wu.at[rows], wsem.at[8 + s]).wait()

    def wait_down(s):
        pltpu.make_async_copy(
            wd_h.at[:, pl.ds(0, 512)], wd.at[pl.ds(0, FFB), pl.ds(s * 512, 512)], wsem.at[16 + s]
        ).wait()

    def rows_of(i):
        return pl.ds(pl.multiple_of(i * RC, RC), RC)

    def ag(n, i):
        return pltpu.make_async_remote_copy(
            src_ref=tok.at[PARENT[n]].at[rows_of(i)], dst_ref=tok.at[n].at[rows_of(i)],
            send_sem=ag_send.at[n, i], recv_sem=ag_recv.at[n, i],
            device_id=near(EDGES[n][1]), device_id_type=MESH,
        )

    def rs(n, i):
        return pltpu.make_async_remote_copy(
            src_ref=part.at[n].at[rows_of(i)], dst_ref=rsr.at[n].at[rows_of(i)],
            send_sem=rs_send.at[n, i], recv_sem=rs_recv.at[n, i],
            device_id=near(EDGES[n][1] ^ 1), device_id_type=MESH,
        )

    def exchange(j):
        to = (p + j) % NPOP
        cols = pl.ds(pl.multiple_of(to * 512, 512), 512)
        return [
            pltpu.make_async_remote_copy(
                src_ref=a, dst_ref=b, send_sem=x_send.at[j, q], recv_sem=x_recv.at[j, q],
                device_id=peer(j), device_id_type=MESH,
            )
            for q, (a, b) in enumerate(
                ((fsend, frecv.at[j]), (rsend, rrecv.at[j]), (lsend.at[:, cols], lrecv.at[j]))
            )
        ]

    own.wait()
    pl.semaphore_wait(bar, 4 + NPOP - 1)
    for i in range(NCH):
        for n in GROUP[0]:
            ag(n, i).start()

    for c in small:
        c.wait()
    fsend[...] = jnp.zeros((8, 128), F32)
    fsend[0:1, 0:8] = fit[...]
    rf[...] = jnp.zeros((16, 512), F32)
    for t, ref in enumerate((gr, ur, dl)):
        for k in range(4):
            rf[4 * k : 4 * k + 4, 0:FFB] = ref[k].astype(F32)
        rsend[16 * t : 16 * t + 16, :] = rf[...].astype(BF)
    for t, ref in enumerate((gl, ul, dr)):
        for k in range(4):
            lf[4 * k : 4 * k + 4, :] = ref[k].astype(F32)
        lsend[16 * t : 16 * t + 16, :] = lf[...].astype(BF)
    for j in range(1, NPOP):
        for c in exchange(j):
            c.start()
    frecv[0] = fsend[...]
    rrecv[0] = rsend[...]
    lrecv[0] = lsend[:, pl.ds(pl.multiple_of(p * 512, 512), 512)]

    zero16 = jnp.zeros((16, 512), BF)
    rxg[...] = jnp.concatenate([rsend[0:16, :], rsend[0:16, :], zero16, zero16], axis=0)
    rxu[...] = jnp.concatenate([zero16, zero16, rsend[16:32, :], rsend[16:32, :]], axis=0)
    dlx[...] = jnp.concatenate([zero16] * 5 + [rsend[32:48, :], rsend[32:48, :], zero16], axis=0)
    for n in range(32):
        cols = pl.ds(pl.multiple_of(source(n) * FB, FB), FB)
        to = pl.ds(n * FB, FB)
        a, b, c = lsend[0:16, cols], lsend[16:32, cols], lsend[32:48, cols]
        lx[:, to] = jnp.concatenate([a, a, b, b], axis=0)
        wd[FFB:512, to] = jnp.concatenate([c, c, jnp.zeros((16, FB), BF)], axis=0)
        gainp[n : n + 1, :] = gain[pl.ds(source(n), 1), :]
    hid[:, 384:512] = jnp.zeros((ROWS, 128), BF)

    def project(s, i):
        rows = rows_of(i)
        blocks, square = [], None
        for n in GROUP[s]:
            t = tok[n, rows, :].astype(F32)
            square = t * t if square is None else square + t * t
            blocks.append((t * gainp[n : n + 1, :]).astype(BF))
        v = jnp.concatenate(blocks, axis=1)
        at = pl.ds(s * 512, 512)
        g, u, q = mm(v, wg[at, :]), mm(v, wu[at, :]), nt(v, lx[:, s * 512 : s * 512 + 512])
        if s == 0:
            accg[rows, :], accu[rows, :], accp[rows, :], sq[rows, :] = g, u, q, square
        else:
            accg[rows, :] += g
            accu[rows, :] += u
            accp[rows, :] += q
            sq[rows, :] += square

    def weighting(i, lanes):
        row = lax.broadcasted_iota(jnp.int32, (RC, lanes), 0) + i * RC
        lane = lax.broadcasted_iota(jnp.int32, (RC, lanes), 1)
        member = row // 64
        sign = (1 - 2 * (member % 2)).astype(F32)
        return jnp.where((lane % 16) // 4 == member // 2, sign, 0.0), lane

    def split(value, first):
        high = value.astype(BF).astype(F32)
        return jnp.where(first, high, value - high).astype(BF)

    def finish(i):
        rows = rows_of(i)
        scale = lax.rsqrt(jnp.sum(sq[rows, :], axis=1, keepdims=True) * (1.0 / D) + 1e-06)
        sign, lane = weighting(i, 64)
        coef = sign * (accp[rows, :] * scale) * (0.5 / math.sqrt(D))
        coef = split(coef, lane % 32 < 16)
        gate = accg[rows, :] * scale + mm(coef, rxg[:, 0:FFB])
        up = accu[rows, :] * scale + mm(coef, rxu[:, 0:FFB])
        hid[rows, 0:FFB] = (gate / (1.0 + jnp.exp(-gate)) * up).astype(BF)
        projected = nt(hid[rows, :], dlx[...])
        sign, lane = weighting(i, 128)
        coef = sign * projected * (0.5 / math.sqrt(FF))
        coef = split(coef, lane < 96)
        tail = hid[rows, 384:512]
        inside = (lane < 80).astype(F32)
        pert = ((lane >= 80) & (lane < 112)).astype(F32)
        hid[rows, 384:512] = jnp.where(
            inside > 0, tail.astype(F32), jnp.where(pert > 0, coef.astype(F32), 0.0)
        ).astype(BF)

    def down(s, i):
        rows = rows_of(i)
        y = mm(hid[rows, :], wd[:, s * 512 : s * 512 + 512])
        for q, n in enumerate(GROUP[s]):
            part[n, rows, :] = y[:, q * FB : (q + 1) * FB].astype(BF)

    def add_children(n, i):
        rows = rows_of(i)
        if CHILDREN[n]:
            total = part[n, rows, :].astype(F32)
            for c in CHILDREN[n]:
                rs(c, i).wait_recv()
                total = total + rsr[c, rows, :].astype(F32)
            return total
        return None

    def shape_weights():
        every = frecv[:, 0, :]
        lane = lax.broadcasted_iota(jnp.int32, (8, 128), 1)
        valid = lane < 8
        center = jnp.sum(jnp.where(valid, every, 0.0)) * (1.0 / 64)
        off = jnp.where(valid, every - center, 0.0)
        var = jnp.sum(off * off) * (1.0 / 64)
        shaped = off * lax.rsqrt(jnp.broadcast_to(var + 1e-05, (8, 128)))
        wide = jnp.broadcast_to(shaped[:, None, :], (8, 16, 128)).reshape(128, 128)
        row = lax.broadcasted_iota(jnp.int32, (128, 128), 0)
        lane = lax.broadcasted_iota(jnp.int32, (128, 128), 1)
        k = (row % 16) // 4
        pick = jnp.where(lane == 2 * k, 1.0, jnp.where(lane == 2 * k + 1, -1.0, 0.0))
        col = jnp.sum(wide * pick, axis=1, keepdims=True) * (1.0 / math.sqrt(128))
        wcol[...] = jnp.broadcast_to(col, (128, 128))

    def step(t, i):
        rows = rows_of(i)
        take = pl.ds(16 * t, 16)
        if t < 2:
            left = lrecv[:, take, rows].reshape(128, 128).astype(F32) * wcol[...]
            left = left.T
            high = left.astype(BF)
            low = (left - high.astype(F32)).astype(BF)
            right = rrecv[:, take, :].reshape(128, 512)
            out = mm(jnp.concatenate([high, low], axis=1), jnp.concatenate([right, right], axis=0))
            (gsb, usb)[t][rows, :] = out[:, 0:FFB].astype(BF)
        else:
            left = rrecv[:, take, rows].reshape(128, 128).astype(F32).T.astype(BF)
            right = lrecv[:, take, :].reshape(128, 512).astype(F32) * wcol[:, 0:1]
            high = right.astype(BF)
            low = (right - high.astype(F32)).astype(BF)
            out = mm(jnp.concatenate([left, left], axis=1), jnp.concatenate([high, low], axis=0))
            dsb[rows, :] = out.astype(BF)

    outs = [
        pltpu.make_async_copy(gsb, gs_h, osem.at[0]),
        pltpu.make_async_copy(usb, us_h, osem.at[1]),
        pltpu.make_async_copy(dsb.at[pl.ds(0, FFB)], ds_h, osem.at[2]),
    ]

    for s in range(1, SLOTS):
        soon = [4 * s + k for k in range(len(TREE[s])) if slot_of(PARENT[4 * s + k]) == s - 1]
        later = [4 * s + k for k in range(len(TREE[s])) if slot_of(PARENT[4 * s + k]) < s - 1]
        for i in range(NCH):
            for n in later:
                ag(n, i).start()
        wait_in(s - 1)

        def relay(i, carry, s=s, soon=soon):
            for n in GROUP[s - 1]:
                ag(n, i).wait_recv()
            for n in soon:
                ag(n, i).start()
            project(s - 1, i)
            return carry

        lax.fori_loop(0, NCH, relay, 0)

    wait_in(SLOTS - 1)
    wait_down(SLOTS - 1)
    wait_down(SLOTS - 2)

    def turn(i, carry):
        for n in GROUP[SLOTS - 1][:3]:
            ag(n, i).wait_recv()
        project(SLOTS - 1, i)
        finish(i)
        down(SLOTS - 1, i)
        for n in GROUP[SLOTS - 1][:3]:
            rs(n, i).start()
        down(SLOTS - 2, i)
        return carry

    lax.fori_loop(0, NCH, turn, 0)

    for j in range(1, NPOP):
        for c in exchange(j):
            c.wait_recv()
    shape_weights()

    for s in reversed(range(SLOTS - 1)):
        if s > 0:
            wait_down(s - 1)

        def reduce(i, carry, s=s):
            for n in GROUP[s]:
                total = add_children(n, i)
                if total is not None:
                    part[n, rows_of(i), :] = total.astype(BF)
                rs(n, i).start()
            if s > 0:
                down(s - 1, i)
            if 3 <= s <= 5:
                step(5 - s, i)
            return carry

        lax.fori_loop(0, NCH, reduce, 0)
        if 3 <= s <= 5:
            outs[5 - s].start()

    def last(i, carry):
        rows = rows_of(i)
        total = add_children(OWN, i) + tok[OWN, rows, :].astype(F32)
        mixed_ref[rows, :] = total.astype(BF)
        return carry

    lax.fori_loop(0, NCH, last, 0)

    def drain(i, carry):
        for n in range(31):
            ag(n, i).wait_send()
            rs(n, i).wait_send()
        return carry

    lax.fori_loop(0, NCH, drain, 0)
    for j in range(1, NPOP):
        for c in exchange(j):
            c.wait_send()
    for c in outs:
        c.wait()


def per_device(tokens, norm_gain, gate_weight, up_weight, down_weight, gate_left, up_left, down_right,
               gate_right, up_right, down_left, fitness):
    vm = pltpu.VMEM
    dma = pltpu.SemaphoreType.DMA
    anywhere = pl.BlockSpec(memory_space=pl.ANY)
    return pl.pallas_call(
        kernel,
        out_shape=(
            jax.ShapeDtypeStruct((ROWS, FB), BF),
            jax.ShapeDtypeStruct((512, FFB), BF),
            jax.ShapeDtypeStruct((512, FFB), BF),
            jax.ShapeDtypeStruct((FFB, 512), BF),
        ),
        in_specs=[anywhere] * 12,
        out_specs=(pl.BlockSpec(memory_space=pltpu.VMEM), anywhere, anywhere, anywhere),
        scratch_shapes=[
            vm((32, ROWS, FB), BF),
            vm((D, FFB), BF),
            vm((D, FFB), BF),
            vm((512, D), BF),
            vm((ROWS, FFB), F32),
            vm((ROWS, FFB), F32),
            vm((ROWS, 64), F32),
            vm((ROWS, FB), F32),
            vm((ROWS, 512), BF),
            vm((32, ROWS, FB), BF),
            vm((31, ROWS, FB), BF),
            vm((4, 4, D), BF),
            vm((4, 4, D), BF),
            vm((4, 4, D), BF),
            vm((4, 4, FFB), BF),
            vm((4, 4, FFB), BF),
            vm((4, 4, FFB), BF),
            vm((16, D), F32),
            vm((16, 512), F32),
            vm((64, D), BF),
            vm((64, 512), BF),
            vm((64, 512), BF),
            vm((128, 512), BF),
            vm((48, D), BF),
            vm((48, 512), BF),
            vm((8, 128), F32),
            vm((8, 48, 512), BF),
            vm((8, 48, 512), BF),
            vm((8, 8, 128), F32),
            vm((32, FB), F32),
            vm((32, FB), F32),
            vm((1, 8), F32),
            vm((128, 128), F32),
            vm((512, FFB), BF),
            vm((512, FFB), BF),
            vm((512, 512), BF),
            dma((24,)),
            dma((9,)),
            dma((3,)),
            dma((31, NCH)),
            dma((31, NCH)),
            dma((31, NCH)),
            dma((31, NCH)),
            dma((8, 3)),
            dma((8, 3)),
        ],
        compiler_params=pltpu.CompilerParams(
            collective_id=0, has_side_effects=True, vmem_limit_bytes=56 << 20
        ),
        cost_estimate=pl.CostEstimate(flops=6_500_000_000, bytes_accessed=14_000_000, transcendentals=250_000),
        name="es_step",
    )(
        tokens, norm_gain.reshape(32, FB), gate_weight, up_weight, down_weight, gate_left, up_left, down_right,
        gate_right, up_right, down_left, fitness.reshape(1, 8),
    )


def solution(mesh):
    in_specs = (
        P("pop", "mp"),
        P(),
        P(None, "mp"),
        P(None, "mp"),
        P("mp", None),
        P("pop", None, None),
        P("pop", None, None),
        P("pop", None, None),
        P("pop", None, "mp"),
        P("pop", None, "mp"),
        P("pop", None, "mp"),
        P("pop"),
    )
    out_specs = (P("pop", "mp"), P("pop", "mp"), P("pop", "mp"), P("mp", "pop"))
    return jax.shard_map(
        per_device, mesh=mesh, in_specs=in_specs, out_specs=out_specs, check_vma=False
    )
```

time: 356 us -> 91 us (0.26)
  waiting for transfers between devices: 252 us -> 0 us
  Pallas kernels: 0 us -> 68.7 us
  blocking collectives: 48.3 us -> 0 us
  matrix products: 21.2 us -> 0 us
  between operations: 16 us -> 0.64 us
  local copies, waits for them, and re-layouts: 10.8 us -> 20.3 us
  other arithmetic: 7.72 us -> 0 us
    psum x1 -> x0, waiting for transfers between devices: 164 us -> none  [total_down(): full_sum = lax.psum(partial_value, 'mp').astype(jnp.float32)]
    all_gather x4 -> x0, waiting for transfers between devices: 85.3 us -> none  [the longest x1 81.4 us: per_device(): whole = lax.all_gather(tokens, 'mp', axis=1, tiled=True)]
    pallas_call x0 -> x1, Pallas kernels: none -> 68.7 us  [per_device(): pl.pallas_call(kernel, out_shape=(jax.ShapeDtypeStruct((ROWS, FB), BF), j...]
    all_gather x3 -> x0, blocking collectives: 38.3 us -> none  [the longest x1 12.8 us: per_device(): lax.all_gather(gate_right, 'pop', axis=0, tiled=True)]
    dot_general x12 -> x0, matrix products: 21.2 us -> none  [the longest x3 7.27 us: perturbed(): jnp.dot(weighting * projected * spread, flat_right, precision=lax.Precisi...]
    unnamed x25 -> x4, local copies, waits for them, and re-layouts: 2.68 us -> 16.3 us
    unnamed x1 -> x0, blocking collectives: 9.99 us -> none
    reshape x6 -> x0, local copies, waits for them, and re-layouts: 5.03 us -> none  [the longest x3 2.62 us: project_rank(): flat_left = left.reshape(-1, left.shape[2])]
  transfers between devices with their start and end apart: 5 -> 0, of which waited for: 3 -> 0; matrix products, arithmetic and copies ran while one was open for 10% -> 0% of each run, Pallas kernels for 0% -> 0%
where the time goes in v1:
time: 91 us; the launch traced here: 89.7 us
  Pallas kernels  68.7 us (75%)
  local copies, waits for them, and re-layouts  20.3 us (22%)
    pallas_call x1, Pallas kernels, per_device(): pl.pallas_call(kernel, out_shape=(jax.ShapeDtypeStruct((ROWS, FB), BF), j...  68.7 us
    unnamed x4, local copies, waits for them, and re-layouts  16.3 us
    pallas_call x2, local copies, waits for them, and re-layouts, per_device(): pl.pallas_call(kernel, out_shape=(jax.ShapeDtypeStruct((ROWS, FB), BF), j...  4.03 us

profile of v1, /device:TPU:8, one launch (start us, length us, event | category | flops | bytes accessed | tf_op | source)
XLA Modules:
  0.0 89.7 jit_solution(11562881747476977585)
XLA Ops:
  0.6 6.4 %copy.16.wg_h = bf16[4096,464]{1,0:T(8,128)(2,1)} copy(bf16[4096,464]{0,1:T(8,128)(2,1)} %param.14) | data formatting | bytes 7602176 | tf_op args[2]
  7.1 6.5 %copy.17.wu_h = bf16[4096,464]{1,0:T(8,128)(2,1)} copy(bf16[4096,464]{0,1:T(8,128)(2,1)} %param.15) | data formatting | bytes 7602176 | tf_op args[3]
  13.6 68.7 %es_step.1 = (bf16[512,128]{1,0:T(8,128)(2,1)}, bf16[512,464]{1,0:T(8,128)(2,1)}, bf16[512,464]{1,0:T(8,128)(2,1)}, bf16[464,512]{1,0:T(8,128)(2,1)}) custom-call(bf16[512,128]{1,0:T(8,128)(2,1)} %tok_h.1, f32[32,128]{1,0:T(8,128)} %bitcast.2, bf16[4096,464]{1,0:T(8,128)(2,1)} %copy.16.wg_h, bf16[4096,464]{1,0:T(8,128)(2,1)} %copy.17.wu_h, ...), custom_call_target="tpu_custom_call" | custom-call | flops 6499999744 | bytes 14000000 | tf_op jit(solution)/shard_map/es_step/pallas_call | solution.py:376
  82.3 2.0 %copy.18 = bf16[512,464]{0,1:T(8,128)(2,1)} copy(bf16[512,464]{1,0:T(8,128)(2,1)} %get-tuple-element.5) | data formatting | bytes 950272 | tf_op jit(solution)/shard_map/es_step/pallas_call | solution.py:376
  84.3 2.0 %copy.19 = bf16[512,464]{0,1:T(8,128)(2,1)} copy(bf16[512,464]{1,0:T(8,128)(2,1)} %get-tuple-element.6) | data formatting | bytes 950272 | tf_op jit(solution)/shard_map/es_step/pallas_call | solution.py:376
  86.3 1.6 %copy.22 = bf16[512,128]{1,0:T(8,128)(2,1)} copy(bf16[512,128]{1,0:T(8,128)(2,1)} %get-tuple-element.12) | data formatting | bytes 262144
  87.9 1.8 %copy.23 = bf16[464,512]{1,0:T(8,128)(2,1)} copy(bf16[464,512]{1,0:T(8,128)(2,1)} %get-tuple-element.15) | data formatting | bytes 950272

commit v2 on v1

--- a/solution.py
+++ b/solution.py
@@ -91,9 +91,10 @@
 
     for s in range(SLOTS):
         for n in GROUP[s]:
-            rows = pl.ds(pl.multiple_of(source(n) * FB, FB), FB)
-            pltpu.make_async_copy(wg_h.at[rows], wg.at[pl.ds(n * FB, FB)], wsem.at[s]).start()
-            pltpu.make_async_copy(wu_h.at[rows], wu.at[pl.ds(n * FB, FB)], wsem.at[8 + s]).start()
+            cols = pl.ds(pl.multiple_of(source(n) * FB, FB), FB)
+            to = pl.ds(n * FB, FB)
+            pltpu.make_async_copy(wg_h.at[:, cols], wg.at[:, to], wsem.at[s]).start()
+            pltpu.make_async_copy(wu_h.at[:, cols], wu.at[:, to], wsem.at[8 + s]).start()
     for s in reversed(range(SLOTS)):
         for n in GROUP[s]:
             cols = pl.ds(pl.multiple_of(source(n) * FB, FB), FB)
@@ -102,9 +103,9 @@
             ).start()
 
     def wait_in(s):
-        rows = pl.ds(s * 512, 512)
-        pltpu.make_async_copy(wg_h.at[pl.ds(0, 512)], wg.at[rows], wsem.at[s]).wait()
-        pltpu.make_async_copy(wu_h.at[pl.ds(0, 512)], wu.at[rows], wsem.at[8 + s]).wait()
+        cols = pl.ds(s * 512, 512)
+        pltpu.make_async_copy(wg_h.at[:, pl.ds(0, 512)], wg.at[:, cols], wsem.at[s]).wait()
+        pltpu.make_async_copy(wu_h.at[:, pl.ds(0, 512)], wu.at[:, cols], wsem.at[8 + s]).wait()
 
     def wait_down(s):
         pltpu.make_async_copy(
@@ -188,8 +189,8 @@
             square = t * t if square is None else square + t * t
             blocks.append((t * gainp[n : n + 1, :]).astype(BF))
         v = jnp.concatenate(blocks, axis=1)
-        at = pl.ds(s * 512, 512)
-        g, u, q = mm(v, wg[at, :]), mm(v, wu[at, :]), nt(v, lx[:, s * 512 : s * 512 + 512])
+        at = slice(s * 512, s * 512 + 512)
+        g, u, q = nt(v, wg[:, at]), nt(v, wu[:, at]), nt(v, lx[:, at])
         if s == 0:
             accg[rows, :], accu[rows, :], accp[rows, :], sq[rows, :] = g, u, q, square
         else:
@@ -264,25 +265,16 @@
     def step(t, i):
         rows = rows_of(i)
         take = pl.ds(16 * t, 16)
-        if t < 2:
-            left = lrecv[:, take, rows].reshape(128, 128).astype(F32) * wcol[...]
-            left = left.T
-            high = left.astype(BF)
-            low = (left - high.astype(F32)).astype(BF)
-            right = rrecv[:, take, :].reshape(128, 512)
-            out = mm(jnp.concatenate([high, low], axis=1), jnp.concatenate([right, right], axis=0))
-            (gsb, usb)[t][rows, :] = out[:, 0:FFB].astype(BF)
-        else:
-            left = rrecv[:, take, rows].reshape(128, 128).astype(F32).T.astype(BF)
-            right = lrecv[:, take, :].reshape(128, 512).astype(F32) * wcol[:, 0:1]
-            high = right.astype(BF)
-            low = (right - high.astype(F32)).astype(BF)
-            out = mm(jnp.concatenate([left, left], axis=1), jnp.concatenate([high, low], axis=0))
-            dsb[rows, :] = out.astype(BF)
+        left = rrecv[:, take, rows].reshape(128, 128).astype(F32).T.astype(BF)
+        right = lrecv[:, take, :].reshape(128, 512).astype(F32) * wcol[:, 0:1]
+        high = right.astype(BF)
+        low = (right - high.astype(F32)).astype(BF)
+        out = mm(jnp.concatenate([left, left], axis=1), jnp.concatenate([high, low], axis=0))
+        (gsb, usb, dsb)[t][rows, :] = out.astype(BF)
 
     outs = [
-        pltpu.make_async_copy(gsb, gs_h, osem.at[0]),
-        pltpu.make_async_copy(usb, us_h, osem.at[1]),
+        pltpu.make_async_copy(gsb.at[pl.ds(0, FFB)], gs_h, osem.at[0]),
+        pltpu.make_async_copy(usb.at[pl.ds(0, FFB)], us_h, osem.at[1]),
         pltpu.make_async_copy(dsb.at[pl.ds(0, FFB)], ds_h, osem.at[2]),
     ]
 
@@ -373,20 +365,20 @@
     vm = pltpu.VMEM
     dma = pltpu.SemaphoreType.DMA
     anywhere = pl.BlockSpec(memory_space=pl.ANY)
-    return pl.pallas_call(
+    mixed, gate_step, up_step, down_step = pl.pallas_call(
         kernel,
         out_shape=(
             jax.ShapeDtypeStruct((ROWS, FB), BF),
-            jax.ShapeDtypeStruct((512, FFB), BF),
-            jax.ShapeDtypeStruct((512, FFB), BF),
+            jax.ShapeDtypeStruct((FFB, 512), BF),
+            jax.ShapeDtypeStruct((FFB, 512), BF),
             jax.ShapeDtypeStruct((FFB, 512), BF),
         ),
         in_specs=[anywhere] * 12,
         out_specs=(pl.BlockSpec(memory_space=pltpu.VMEM), anywhere, anywhere, anywhere),
         scratch_shapes=[
             vm((32, ROWS, FB), BF),
-            vm((D, FFB), BF),
-            vm((D, FFB), BF),
+            vm((FFB, D), BF),
+            vm((FFB, D), BF),
             vm((512, D), BF),
             vm((ROWS, FFB), F32),
             vm((ROWS, FFB), F32),
@@ -417,8 +409,8 @@
             vm((32, FB), F32),
             vm((1, 8), F32),
             vm((128, 128), F32),
-            vm((512, FFB), BF),
-            vm((512, FFB), BF),
+            vm((512, 512), BF),
+            vm((512, 512), BF),
             vm((512, 512), BF),
             dma((24,)),
             dma((9,)),
@@ -436,9 +428,36 @@
         cost_estimate=pl.CostEstimate(flops=6_500_000_000, bytes_accessed=14_000_000, transcendentals=250_000),
         name="es_step",
     )(
-        tokens, norm_gain.reshape(32, FB), gate_weight, up_weight, down_weight, gate_left, up_left, down_right,
+        tokens, norm_gain.reshape(32, FB), gate_weight.T, up_weight.T, down_weight, gate_left, up_left, down_right,
         gate_right, up_right, down_left, fitness.reshape(1, 8),
     )
+    mixed, gate_step, up_step, down_step = hand_over(mixed, gate_step, up_step, down_step)
+    return mixed, gate_step.T, up_step.T, down_step
+
+
+def move(a, b, c, d, a_out, b_out, c_out, d_out, a_mid, b_mid, c_mid, d_mid, sem):
+    steps = (((a, a_mid), (a_mid, a_out)), ((b, b_mid), (b_mid, b_out)), ((c, c_mid), (c_mid, c_out)), ((d, d_mid), (d_mid, d_out)))
+    first = [pltpu.make_async_copy(*one, sem.at[0, n]) for n, (one, _) in enumerate(steps)]
+    second = [pltpu.make_async_copy(*two, sem.at[1, n]) for n, (_, two) in enumerate(steps)]
+    for c in first:
+        c.start()
+    for c, d in zip(first, second):
+        c.wait()
+        d.start()
+    for d in second:
+        d.wait()
+
+
+def hand_over(*arrays):
+    anywhere = pl.BlockSpec(memory_space=pl.ANY)
+    return pl.pallas_call(
+        move,
+        out_shape=tuple(jax.ShapeDtypeStruct(a.shape, a.dtype) for a in arrays),
+        in_specs=[anywhere] * 4,
+        out_specs=(anywhere,) * 4,
+        scratch_shapes=[pltpu.VMEM(a.shape, a.dtype) for a in arrays] + [pltpu.SemaphoreType.DMA((2, 4))],
+        name="hand_over",
+    )(*arrays)
 
 
 def solution(mesh):

time: 91 us -> 73.3 us (0.81); the launches traced: 89.7 us -> 72.9 us
  local copies, waits for them, and re-layouts: 20.3 us -> 0 us
  Pallas kernels: 68.7 us -> 72.3 us
    unnamed x4 -> x0, local copies, waits for them, and re-layouts: 16.3 us -> none
    pallas_call x2 -> x0, local copies, waits for them, and re-layouts: 4.03 us -> none  [per_device(): pl.pallas_call(kernel, out_shape=(jax.ShapeDtypeStruct((ROWS, FB), BF), j...]
    pallas_call x0 -> x1, Pallas kernels: none -> 2.25 us  [hand_over(): pl.pallas_call(move, out_shape=tuple((jax.ShapeDtypeStruct(a.shape, a.dty...]
    pallas_call x1, Pallas kernels: 68.7 us -> 70 us  [per_device(): pl.pallas_call(kernel, out_shape=(jax.ShapeDtypeStruct((ROWS, FB), BF), j...]
where the time goes in v2:
time: 73.3 us; the launch traced here: 72.9 us
  Pallas kernels  72.3 us (99%)
    pallas_call x1, Pallas kernels, per_device(): pl.pallas_call(kernel, out_shape=(jax.ShapeDtypeStruct((ROWS, FB), BF), j...  70 us
    pallas_call x1, Pallas kernels, hand_over(): pl.pallas_call(move, out_shape=tuple((jax.ShapeDtypeStruct(a.shape, a.dty...  2.25 us

profile of v2, /device:TPU:8, one launch (start us, length us, event | category | flops | bytes accessed | tf_op | source)
XLA Modules:
  0.0 72.9 jit_solution(4299305846881688098)
XLA Ops:
  0.6 70.0 %es_step.1 = (bf16[512,128]{1,0:T(8,128)(2,1)}, bf16[464,512]{1,0:T(8,128)(2,1)}, bf16[464,512]{1,0:T(8,128)(2,1)}, bf16[464,512]{1,0:T(8,128)(2,1)}) custom-call(bf16[512,128]{1,0:T(8,128)(2,1)} %tok_h.1, f32[32,128]{1,0:T(8,128)} %bitcast.10, bf16[464,4096]{1,0:T(8,128)(2,1)} %bitcast.6, bf16[464,4096]{1,0:T(8,128)(2,1)} %bitcast.7, ...), custom_call_target="tpu_custom_call" | custom-call | flops 6499999744 | bytes 14000000 | tf_op jit(solution)/shard_map/es_step/pallas_call | solution.py:368
  70.7 2.3 %hand_over.1 = (bf16[512,128]{1,0:T(8,128)(2,1)}, bf16[464,512]{1,0:T(8,128)(2,1)}, bf16[464,512]{1,0:T(8,128)(2,1)}, bf16[464,512]{1,0:T(8,128)(2,1)}) custom-call(bf16[512,128]{1,0:T(8,128)(2,1)} %get-tuple-element.12.a, bf16[464,512]{1,0:T(8,128)(2,1)} %get-tuple-element.13.b, bf16[464,512]{1,0:T(8,128)(2,1)} %get-tuple-element.14.c, ...), custom_call_target="tpu_custom_call" | custom-call | tf_op jit(solution)/shard_map/hand_over/pallas_call | solution.py:453

commit v3 on v2

--- a/solution.py
+++ b/solution.py
@@ -15,25 +15,36 @@
 ROWS, FB, FFB, D, FF = 512, 128, 464, 4096, 14848
 NCH = 4
 RC = ROWS // NCH
+HALF = ROWS // 2
 SLOTS = 8
 OWN = 31
 
 TREE = (
-    (((0, 0), (1, 0)), ((0, 0), (3, 0)), ((0, 0), (0, 1)), ((0, 0), (0, 7))),
-    (((1, 0), (2, 0)), ((0, 7), (3, 7)), ((1, 0), (1, 1)), ((0, 7), (0, 6))),
-    (((0, 7), (1, 7)), ((0, 1), (3, 1)), ((0, 1), (0, 2)), ((0, 6), (0, 5))),
-    (((0, 6), (1, 6)), ((0, 6), (3, 6)), ((2, 0), (2, 1)), ((0, 5), (0, 4))),
-    (((0, 5), (1, 5)), ((0, 2), (3, 2)), ((1, 1), (1, 2)), ((2, 0), (2, 7))),
-    (((0, 4), (1, 4)), ((3, 6), (2, 6)), ((2, 1), (2, 2)), ((0, 4), (0, 3))),
-    (((1, 5), (2, 5)), ((0, 4), (3, 4)), ((1, 2), (1, 3)), ((3, 6), (3, 5))),
-    (((1, 4), (2, 4)), ((0, 3), (3, 3)), ((2, 2), (2, 3))),
+    ((0, (0, 0), (1, 0)), (1, (0, 0), (3, 0)), (2, (0, 0), (0, 1)), (3, (0, 0), (0, 7))),
+    ((0, (0, 1), (1, 1)), (1, (0, 7), (3, 7)), (2, (3, 0), (3, 1)), (3, (0, 7), (0, 6))),
+    ((0, (0, 6), (1, 6)), (1, (3, 0), (2, 0)), (2, (0, 1), (0, 2)), (3, (1, 0), (1, 7))),
+    ((0, (1, 1), (2, 1)), (1, (3, 7), (2, 7)), (2, (1, 1), (1, 2)), (3, (0, 6), (0, 5))),
+    ((0, (1, 6), (2, 6)), (1, (0, 6), (3, 6)), (2, (0, 2), (0, 3)), (3, (1, 6), (1, 5))),
+    ((0, (1, 5), (2, 5)), (1, (0, 5), (3, 5)), (2, (2, 1), (2, 2)), (3, (0, 5), (0, 4))),
+    ((0, (0, 3), (1, 3)), (1, (0, 3), (3, 3)), (2, (3, 1), (3, 2)), (3, (1, 5), (1, 4))),
+    ((1, (0, 4), (3, 4)), (2, (2, 2), (2, 3)), (3, (2, 5), (2, 4))),
 )
-EDGES = [(s, k) + e for s, slot in enumerate(TREE) for k, e in enumerate(slot)]
+EDGES = [(s,) + e for s, slot in enumerate(TREE) for e in slot]
 OFFSET = [e[3] for e in EDGES] + [(0, 0)]
 INDEX = {o: n for n, o in enumerate(OFFSET)}
 PARENT = [INDEX[e[2]] for e in EDGES]
 CHILDREN = [[c for c in range(31) if PARENT[c] == n] for n in range(32)]
 GROUP = [list(range(4 * s, 4 * s + 4)) for s in range(SLOTS)]
+EDGE_GROUP = [[n for n in g if n != OWN] for g in GROUP]
+
+ORDER = (
+    "SA0", "SB0", "SA1", "SB1", "PA0", "SA2", "SA3", "SB2", "PA1", "PB1", "SA4", "SB3", "PA2", "PA3",
+    "SB4", "PB2", "SA5", "SA6", "PB3", "PA4", "SB5", "PB4", "SA7", "SB6", "PB0", "PA5", "PA6", "SB7",
+    "PB5", "PA7", "FA0", "DA7", "RA7", "DA6", "PB6", "RA6", "PB7", "FB0", "DB7", "RB7", "DA5", "DB6",
+    "RA5", "DB5", "DA2", "RB6", "XA0", "DA3", "DA4", "RB5", "RA4", "RA3", "DB3", "DB4", "RB4", "DB1",
+    "DA1", "RA2", "RB3", "DB2", "DA0", "RB2", "TA1", "RA1", "RB1", "DB0", "RA0", "RB0", "TA0", "TA2",
+    "LA0", "LB0",
+)
 
 
 def slot_of(n):
@@ -88,6 +99,51 @@
         pl.semaphore_signal(bar, inc=1, device_id=near(k), device_id_type=MESH)
     for j in range(1, NPOP):
         pl.semaphore_signal(bar, inc=1, device_id=peer(j), device_id_type=MESH)
+
+    def wait_in(s):
+        cols = pl.ds(s * 512, 512)
+        pltpu.make_async_copy(wg_h.at[:, pl.ds(0, 512)], wg.at[:, cols], wsem.at[s]).wait()
+        pltpu.make_async_copy(wu_h.at[:, pl.ds(0, 512)], wu.at[:, cols], wsem.at[8 + s]).wait()
+
+    def wait_down(s):
+        pltpu.make_async_copy(
+            wd_h.at[:, pl.ds(0, 512)], wd.at[pl.ds(0, FFB), pl.ds(s * 512, 512)], wsem.at[16 + s]
+        ).wait()
+
+    def rows_of(i):
+        return pl.ds(pl.multiple_of(i * RC, RC), RC)
+
+    def ag(n, i):
+        return pltpu.make_async_remote_copy(
+            src_ref=(tok_h if PARENT[n] == OWN else tok.at[PARENT[n]]).at[rows_of(i)], dst_ref=tok.at[n].at[rows_of(i)],
+            send_sem=ag_send, recv_sem=ag_recv.at[n, i],
+            device_id=near(EDGES[n][1]), device_id_type=MESH,
+        )
+
+    def rs(n, i):
+        return pltpu.make_async_remote_copy(
+            src_ref=part.at[n].at[rows_of(i)], dst_ref=rsr.at[n].at[rows_of(i)],
+            send_sem=rs_send, recv_sem=rs_recv.at[n, i],
+            device_id=near(EDGES[n][1] ^ 1), device_id_type=MESH,
+        )
+
+    def exchange(j):
+        to = (p + j) % NPOP
+        cols = pl.ds(pl.multiple_of(to * 512, 512), 512)
+        return [
+            pltpu.make_async_remote_copy(
+                src_ref=a, dst_ref=b, send_sem=x_send.at[j, q], recv_sem=x_recv.at[j, q],
+                device_id=peer(j), device_id_type=MESH,
+            )
+            for q, (a, b) in enumerate(
+                ((fsend, frecv.at[j]), (rsend, rrecv.at[j]), (lsend.at[:, cols], lrecv.at[j]))
+            )
+        ]
+
+    pl.semaphore_wait(bar, 4 + NPOP - 1)
+    for i in range(NCH):
+        for n in EDGE_GROUP[0]:
+            ag(n, i).start()
 
     for s in range(SLOTS):
         for n in GROUP[s]:
@@ -102,51 +158,8 @@
                 wd_h.at[:, cols], wd.at[pl.ds(0, FFB), pl.ds(n * FB, FB)], wsem.at[16 + s]
             ).start()
 
-    def wait_in(s):
-        cols = pl.ds(s * 512, 512)
-        pltpu.make_async_copy(wg_h.at[:, pl.ds(0, 512)], wg.at[:, cols], wsem.at[s]).wait()
-        pltpu.make_async_copy(wu_h.at[:, pl.ds(0, 512)], wu.at[:, cols], wsem.at[8 + s]).wait()
-
-    def wait_down(s):
-        pltpu.make_async_copy(
-            wd_h.at[:, pl.ds(0, 512)], wd.at[pl.ds(0, FFB), pl.ds(s * 512, 512)], wsem.at[16 + s]
-        ).wait()
-
-    def rows_of(i):
-        return pl.ds(pl.multiple_of(i * RC, RC), RC)
-
-    def ag(n, i):
-        return pltpu.make_async_remote_copy(
-            src_ref=tok.at[PARENT[n]].at[rows_of(i)], dst_ref=tok.at[n].at[rows_of(i)],
-            send_sem=ag_send.at[n, i], recv_sem=ag_recv.at[n, i],
-            device_id=near(EDGES[n][1]), device_id_type=MESH,
-        )
-
-    def rs(n, i):
-        return pltpu.make_async_remote_copy(
-            src_ref=part.at[n].at[rows_of(i)], dst_ref=rsr.at[n].at[rows_of(i)],
-            send_sem=rs_send.at[n, i], recv_sem=rs_recv.at[n, i],
-            device_id=near(EDGES[n][1] ^ 1), device_id_type=MESH,
-        )
-
-    def exchange(j):
-        to = (p + j) % NPOP
-        cols = pl.ds(pl.multiple_of(to * 512, 512), 512)
-        return [
-            pltpu.make_async_remote_copy(
-                src_ref=a, dst_ref=b, send_sem=x_send.at[j, q], recv_sem=x_recv.at[j, q],
-                device_id=peer(j), device_id_type=MESH,
-            )
-            for q, (a, b) in enumerate(
-                ((fsend, frecv.at[j]), (rsend, rrecv.at[j]), (lsend.at[:, cols], lrecv.at[j]))
-            )
-        ]
 
     own.wait()
-    pl.semaphore_wait(bar, 4 + NPOP - 1)
-    for i in range(NCH):
-        for n in GROUP[0]:
-            ag(n, i).start()
 
     for c in small:
         c.wait()
@@ -181,8 +194,8 @@
         gainp[n : n + 1, :] = gain[pl.ds(source(n), 1), :]
     hid[:, 384:512] = jnp.zeros((ROWS, 128), BF)
 
-    def project(s, i):
-        rows = rows_of(i)
+    def project(s, h, first):
+        rows = slice(h * HALF, h * HALF + HALF)
         blocks, square = [], None
         for n in GROUP[s]:
             t = tok[n, rows, :].astype(F32)
@@ -191,7 +204,7 @@
         v = jnp.concatenate(blocks, axis=1)
         at = slice(s * 512, s * 512 + 512)
         g, u, q = nt(v, wg[:, at]), nt(v, wu[:, at]), nt(v, lx[:, at])
-        if s == 0:
+        if first:
             accg[rows, :], accu[rows, :], accp[rows, :], sq[rows, :] = g, u, q, square
         else:
             accg[rows, :] += g
@@ -199,9 +212,9 @@
             accp[rows, :] += q
             sq[rows, :] += square
 
-    def weighting(i, lanes):
-        row = lax.broadcasted_iota(jnp.int32, (RC, lanes), 0) + i * RC
-        lane = lax.broadcasted_iota(jnp.int32, (RC, lanes), 1)
+    def weighting(h, lanes):
+        row = lax.broadcasted_iota(jnp.int32, (HALF, lanes), 0) + h * HALF
+        lane = lax.broadcasted_iota(jnp.int32, (HALF, lanes), 1)
         member = row // 64
         sign = (1 - 2 * (member % 2)).astype(F32)
         return jnp.where((lane % 16) // 4 == member // 2, sign, 0.0), lane
@@ -210,17 +223,17 @@
         high = value.astype(BF).astype(F32)
         return jnp.where(first, high, value - high).astype(BF)
 
-    def finish(i):
-        rows = rows_of(i)
+    def finish(h, s):
+        rows = slice(h * HALF, h * HALF + HALF)
         scale = lax.rsqrt(jnp.sum(sq[rows, :], axis=1, keepdims=True) * (1.0 / D) + 1e-06)
-        sign, lane = weighting(i, 64)
+        sign, lane = weighting(h, 64)
         coef = sign * (accp[rows, :] * scale) * (0.5 / math.sqrt(D))
         coef = split(coef, lane % 32 < 16)
         gate = accg[rows, :] * scale + mm(coef, rxg[:, 0:FFB])
         up = accu[rows, :] * scale + mm(coef, rxu[:, 0:FFB])
         hid[rows, 0:FFB] = (gate / (1.0 + jnp.exp(-gate)) * up).astype(BF)
         projected = nt(hid[rows, :], dlx[...])
-        sign, lane = weighting(i, 128)
+        sign, lane = weighting(h, 128)
         coef = sign * projected * (0.5 / math.sqrt(FF))
         coef = split(coef, lane < 96)
         tail = hid[rows, 384:512]
@@ -230,8 +243,8 @@
             inside > 0, tail.astype(F32), jnp.where(pert > 0, coef.astype(F32), 0.0)
         ).astype(BF)
 
-    def down(s, i):
-        rows = rows_of(i)
+    def down(s, h):
+        rows = slice(h * HALF, h * HALF + HALF)
         y = mm(hid[rows, :], wd[:, s * 512 : s * 512 + 512])
         for q, n in enumerate(GROUP[s]):
             part[n, rows, :] = y[:, q * FB : (q + 1) * FB].astype(BF)
@@ -278,81 +291,100 @@
         pltpu.make_async_copy(dsb.at[pl.ds(0, FFB)], ds_h, osem.at[2]),
     ]
 
-    for s in range(1, SLOTS):
-        soon = [4 * s + k for k in range(len(TREE[s])) if slot_of(PARENT[4 * s + k]) == s - 1]
-        later = [4 * s + k for k in range(len(TREE[s])) if slot_of(PARENT[4 * s + k]) < s - 1]
-        for i in range(NCH):
-            for n in later:
+    seen, ready_in, ready_down, begun = set(), set(), set(), set()
+
+    def halves(h, body):
+        def run(c, carry):
+            body(2 * h + c)
+            return carry
+
+        lax.fori_loop(0, 2, run, 0)
+
+    def arrive(h, blocks):
+        new = [n for n in blocks if n != OWN and (h, n) not in seen]
+        seen.update((h, n) for n in new)
+        return new
+
+    def send_slot(h, s):
+        wait = {n: arrive(h, [PARENT[n]]) for n in EDGE_GROUP[s]}
+
+        def body(i):
+            for n in EDGE_GROUP[s]:
+                for q in wait[n]:
+                    ag(q, i).wait_recv()
                 ag(n, i).start()
-        wait_in(s - 1)
-
-        def relay(i, carry, s=s, soon=soon):
-            for n in GROUP[s - 1]:
+
+        halves(h, body)
+
+    def project_slot(h, s):
+        if s not in ready_in:
+            ready_in.add(s)
+            wait_in(s)
+        new, first = arrive(h, GROUP[s]), h not in begun
+        begun.add(h)
+
+        def body(i):
+            for n in new:
                 ag(n, i).wait_recv()
-            for n in soon:
-                ag(n, i).start()
-            project(s - 1, i)
-            return carry
-
-        lax.fori_loop(0, NCH, relay, 0)
-
-    wait_in(SLOTS - 1)
-    wait_down(SLOTS - 1)
-    wait_down(SLOTS - 2)
-
-    def turn(i, carry):
-        for n in GROUP[SLOTS - 1][:3]:
-            ag(n, i).wait_recv()
-        project(SLOTS - 1, i)
-        finish(i)
-        down(SLOTS - 1, i)
-        for n in GROUP[SLOTS - 1][:3]:
-            rs(n, i).start()
-        down(SLOTS - 2, i)
-        return carry
-
-    lax.fori_loop(0, NCH, turn, 0)
-
-    for j in range(1, NPOP):
-        for c in exchange(j):
-            c.wait_recv()
-    shape_weights()
-
-    for s in reversed(range(SLOTS - 1)):
-        if s > 0:
-            wait_down(s - 1)
-
-        def reduce(i, carry, s=s):
-            for n in GROUP[s]:
+
+        halves(h, body)
+        project(s, h, first)
+
+    def down_slot(h, s):
+        if s not in ready_down:
+            ready_down.add(s)
+            wait_down(s)
+        down(s, h)
+
+    def reduce_slot(h, s):
+        def body(i):
+            for n in EDGE_GROUP[s]:
                 total = add_children(n, i)
                 if total is not None:
                     part[n, rows_of(i), :] = total.astype(BF)
                 rs(n, i).start()
-            if s > 0:
-                down(s - 1, i)
-            if 3 <= s <= 5:
-                step(5 - s, i)
+
+        halves(h, body)
+
+    def last(h, s):
+        def body(i):
+            rows = rows_of(i)
+            total = add_children(OWN, i) + tok[OWN, rows, :].astype(F32)
+            mixed_ref[rows, :] = total.astype(BF)
+
+        halves(h, body)
+
+    def weights_ready(h, s):
+        for j in range(1, NPOP):
+            for c in exchange(j):
+                c.wait_recv()
+        shape_weights()
+
+    def step_slot(h, t):
+        def run(i, carry):
+            step(t, i)
             return carry
 
-        lax.fori_loop(0, NCH, reduce, 0)
-        if 3 <= s <= 5:
-            outs[5 - s].start()
-
-    def last(i, carry):
-        rows = rows_of(i)
-        total = add_children(OWN, i) + tok[OWN, rows, :].astype(F32)
-        mixed_ref[rows, :] = total.astype(BF)
-        return carry
-
-    lax.fori_loop(0, NCH, last, 0)
-
-    def drain(i, carry):
-        for n in range(31):
-            ag(n, i).wait_send()
-            rs(n, i).wait_send()
-        return carry
-
-    lax.fori_loop(0, NCH, drain, 0)
+        lax.fori_loop(0, NCH, run, 0)
+        outs[t].start()
+
+    tasks = {
+        "S": send_slot, "P": project_slot, "F": finish, "D": down_slot,
+        "R": reduce_slot, "L": last, "X": weights_ready, "T": step_slot,
+    }
+    for word in ORDER[2:]:
+        tasks[word[0]]("AB".index(word[1]), int(word[2]))
+
+    ag_all = pltpu.make_async_remote_copy(
+        src_ref=tok.at[pl.ds(0, OWN)], dst_ref=tok.at[pl.ds(0, OWN)], send_sem=ag_send, recv_sem=ag_recv.at[0, 0],
+        device_id=near(0), device_id_type=MESH,
+    )
+    rs_all = pltpu.make_async_remote_copy(
+        src_ref=part.at[pl.ds(0, OWN)], dst_ref=rsr, send_sem=rs_send, recv_sem=rs_recv.at[0, 0],
+        device_id=near(0), device_id_type=MESH,
+    )
+    ag_all.wait_send()
+    rs_all.wait_send()
     for j in range(1, NPOP):
         for c in exchange(j):
             c.wait_send()
@@ -415,9 +447,9 @@
             dma((24,)),
             dma((9,)),
             dma((3,)),
+            dma,
             dma((31, NCH)),
-            dma((31, NCH)),
-            dma((31, NCH)),
+            dma,
             dma((31, NCH)),
             dma((8, 3)),
             dma((8, 3)),

time: 73.3 us -> 66.5 us (0.907)
  Pallas kernels: 72.3 us -> 65.7 us
    pallas_call x1, Pallas kernels: 70 us -> 63.5 us  [per_device(): pl.pallas_call(kernel, out_shape=(jax.ShapeDtypeStruct((ROWS, FB), BF), j...]
where the time goes in v3:
time: 66.5 us; the launch traced here: 66.4 us
  Pallas kernels  65.7 us (99%)
    pallas_call x1, Pallas kernels, per_device(): pl.pallas_call(kernel, out_shape=(jax.ShapeDtypeStruct((ROWS, FB), BF), j...  63.5 us
    pallas_call x1, Pallas kernels, hand_over(): pl.pallas_call(move, out_shape=tuple((jax.ShapeDtypeStruct(a.shape, a.dty...  2.25 us

profile of v3, /device:TPU:8, one launch (start us, length us, event | category | flops | bytes accessed | tf_op | source)
XLA Modules:
  0.0 66.4 jit_solution(3609375770004665561)
XLA Ops:
  0.6 63.5 %es_step.1 = (bf16[512,128]{1,0:T(8,128)(2,1)}, bf16[464,512]{1,0:T(8,128)(2,1)}, bf16[464,512]{1,0:T(8,128)(2,1)}, bf16[464,512]{1,0:T(8,128)(2,1)}) custom-call(bf16[512,128]{1,0:T(8,128)(2,1)} %tok_h.1, f32[32,128]{1,0:T(8,128)} %bitcast.10, bf16[464,4096]{1,0:T(8,128)(2,1)} %bitcast.6, bf16[464,4096]{1,0:T(8,128)(2,1)} %bitcast.7, ...), custom_call_target="tpu_custom_call" | custom-call | flops 6499999744 | bytes 14000000 | tf_op jit(solution)/shard_map/es_step/pallas_call | solution.py:400
  64.1 2.3 %hand_over.1 = (bf16[512,128]{1,0:T(8,128)(2,1)}, bf16[464,512]{1,0:T(8,128)(2,1)}, bf16[464,512]{1,0:T(8,128)(2,1)}, bf16[464,512]{1,0:T(8,128)(2,1)}) custom-call(bf16[512,128]{1,0:T(8,128)(2,1)} %get-tuple-element.12.a, bf16[464,512]{1,0:T(8,128)(2,1)} %get-tuple-element.13.b, bf16[464,512]{1,0:T(8,128)(2,1)} %get-tuple-element.14.c, ...), custom_call_target="tpu_custom_call" | custom-call | tf_op jit(solution)/shard_map/hand_over/pallas_call | solution.py:485

commit v4 on v3

--- a/solution.py
+++ b/solution.py
@@ -17,38 +17,39 @@
 RC = ROWS // NCH
 HALF = ROWS // 2
 SLOTS = 8
+
+TREE = (
+    ((1, 0), 0, 1, 31), ((3, 0), 1, 1, 31), ((0, 1), 2, 1, 31), ((0, 7), 3, 1, 31),
+    ((1, 1), 0, 1, 2), ((3, 7), 1, 1, 3), ((3, 1), 2, 1, 1), ((0, 6), 3, 1, 3),
+    ((1, 6), 0, 1, 7), ((2, 0), 1, 1, 1), ((0, 2), 2, 1, 2), ((0, 5), 3, 1, 7),
+    ((2, 1), 0, 1, 4), ((3, 6), 1, 1, 7), ((1, 2), 2, 1, 4), ((1, 7), 3, 1, 0),
+    ((2, 6), 0, 1, 8), ((2, 7), 1, 1, 5), ((0, 3), 2, 1, 10), ((1, 5), 3, 1, 8),
+    ((1, 3), 0, 1, 18), ((3, 5), 1, 1, 11), ((2, 2), 2, 1, 12), ((1, 4), 3, 1, 19),
+    ((2, 5), 0, 1, 19), ((3, 3), 1, 1, 18), ((3, 2), 2, 1, 6), ((0, 4), 3, 1, 11),
+    ((2, 3), 1, 1, 25), ((3, 4), 2, 1, 25), ((2, 4), 3, 1, 24),
+)
 OWN = 31
-
-TREE = (
-    ((0, (0, 0), (1, 0)), (1, (0, 0), (3, 0)), (2, (0, 0), (0, 1)), (3, (0, 0), (0, 7))),
-    ((0, (0, 1), (1, 1)), (1, (0, 7), (3, 7)), (2, (3, 0), (3, 1)), (3, (0, 7), (0, 6))),
-    ((0, (0, 6), (1, 6)), (1, (3, 0), (2, 0)), (2, (0, 1), (0, 2)), (3, (1, 0), (1, 7))),
-    ((0, (1, 1), (2, 1)), (1, (3, 7), (2, 7)), (2, (1, 1), (1, 2)), (3, (0, 6), (0, 5))),
-    ((0, (1, 6), (2, 6)), (1, (0, 6), (3, 6)), (2, (0, 2), (0, 3)), (3, (1, 6), (1, 5))),
-    ((0, (1, 5), (2, 5)), (1, (0, 5), (3, 5)), (2, (2, 1), (2, 2)), (3, (0, 5), (0, 4))),
-    ((0, (0, 3), (1, 3)), (1, (0, 3), (3, 3)), (2, (3, 1), (3, 2)), (3, (1, 5), (1, 4))),
-    ((1, (0, 4), (3, 4)), (2, (2, 2), (2, 3)), (3, (2, 5), (2, 4))),
+OFFSET = [e[0] for e in TREE] + [(0, 0)]
+PARENT = [e[3] for e in TREE]
+CHILDREN = [[c for c in range(OWN) if PARENT[c] == n] for n in range(32)]
+GROUP = [list(range(4 * s, 4 * s + 4)) for s in range(SLOTS)]
+REACH = sorted({(e[1], e[2]) for e in TREE} | {(e[1] ^ 1, e[2]) for e in TREE})
+
+ORDER = (
+    "SA3", "SA2", "SB3", "SA1", "SA0", "SB0", "SB1", "SB2", "KA0", "SA7", "SA10", "SA9", "SA4", "SB7",
+    "SB10", "SA5", "SB4", "SA15", "SA6", "SB5", "PB0", "SA8", "SA11", "SB9", "SA18", "SB8", "SB6", "SA13",
+    "SB11", "PA0", "SA12", "SB13", "SB18", "SA19", "SB12", "PA1", "SA14", "SB14", "SA25", "SB19", "SA20", "SA27",
+    "SB15", "SA17", "PA2", "SA26", "PB1", "SA24", "SA16", "SA23", "SB25", "PB2", "SA21", "SA22", "SA28", "SA29",
+    "SB24", "PA3", "SB16", "SB20", "SB26", "SA30", "SB27", "SB23", "SB17", "SB21", "PB3", "PA4", "SB28", "SB22",
+    "SB29", "XA0", "SB30", "PA6", "PA5", "PA7", "FA0", "DA7", "RA30", "DA5", "RA28", "RA21", "RA22", "RA20",
+    "RA29", "RA23", "DA6", "PB6", "RA27", "PB5", "DA4", "PB4", "RA16", "RA17", "RA26", "PB7", "FB0", "DB7",
+    "RB30", "RB28", "RB29", "DB6", "DB0", "DB5", "DB4", "RB22", "RA24", "DB3", "RB23", "DB1", "DA3", "RA25",
+    "RB26", "RB21", "RB20", "DA2", "RA11", "RA13", "RB14", "RA14", "RB27", "RB24", "DB2", "RB25", "DA0", "RB9",
+    "RB16", "RA19", "RA12", "RA18", "DA1", "RB12", "RA6", "RB19", "RA15", "TA0", "RB17", "RB11", "RB15", "RA9",
+    "RA8", "RB18", "RB6", "RB13", "RA5", "RB8", "RA4", "RB4", "RA10", "RB5", "RA7", "RB10", "RA1", "RB7",
+    "RB1", "RA0", "RA2", "RA3", "RB0", "RB2", "RB3", "TA1", "LA0", "TA2", "LB0",
 )
-EDGES = [(s,) + e for s, slot in enumerate(TREE) for e in slot]
-OFFSET = [e[3] for e in EDGES] + [(0, 0)]
-INDEX = {o: n for n, o in enumerate(OFFSET)}
-PARENT = [INDEX[e[2]] for e in EDGES]
-CHILDREN = [[c for c in range(31) if PARENT[c] == n] for n in range(32)]
-GROUP = [list(range(4 * s, 4 * s + 4)) for s in range(SLOTS)]
-EDGE_GROUP = [[n for n in g if n != OWN] for g in GROUP]
-
-ORDER = (
-    "SA0", "SB0", "SA1", "SB1", "PA0", "SA2", "SA3", "SB2", "PA1", "PB1", "SA4", "SB3", "PA2", "PA3",
-    "SB4", "PB2", "SA5", "SA6", "PB3", "PA4", "SB5", "PB4", "SA7", "SB6", "PB0", "PA5", "PA6", "SB7",
-    "PB5", "PA7", "FA0", "DA7", "RA7", "DA6", "PB6", "RA6", "PB7", "FB0", "DB7", "RB7", "DA5", "DB6",
-    "RA5", "DB5", "DA2", "RB6", "XA0", "DA3", "DA4", "RB5", "RA4", "RA3", "DB3", "DB4", "RB4", "DB1",
-    "DA1", "RA2", "RB3", "DB2", "DA0", "RB2", "TA1", "RA1", "RB1", "DB0", "RA0", "RB0", "TA0", "TA2",
-    "LA0", "LB0",
-)
-
-
-def slot_of(n):
-    return -1 if n == OWN else n // 4
+ROOTS = max(at for at in range(12) if ORDER[at][0] == "S" and PARENT[int(ORDER[at][2:])] == OWN)
 
 
 def nt(a, b):
@@ -71,10 +72,10 @@
     m = lax.axis_index("mp")
     x, z = m // NZ, m % NZ
 
-    def near(k):
+    def near(k, hops):
         if k < 2:
-            return (p, ((x + (1, NX - 1)[k]) % NX) * NZ + z)
-        return (p, x * NZ + (z + (1, NZ - 1)[k - 2]) % NZ)
+            return (p, ((x + (hops, NX - hops)[k]) % NX) * NZ + z)
+        return (p, x * NZ + (z + (hops, NZ - hops)[k - 2]) % NZ)
 
     def source(n):
         dx, dz = OFFSET[n]
@@ -95,8 +96,8 @@
         c.start()
 
     bar = pltpu.get_barrier_semaphore()
-    for k in range(4):
-        pl.semaphore_signal(bar, inc=1, device_id=near(k), device_id_type=MESH)
+    for k, hops in REACH:
+        pl.semaphore_signal(bar, inc=1, device_id=near(k, hops), device_id_type=MESH)
     for j in range(1, NPOP):
         pl.semaphore_signal(bar, inc=1, device_id=peer(j), device_id_type=MESH)
 
@@ -117,14 +118,14 @@
         return pltpu.make_async_remote_copy(
             src_ref=(tok_h if PARENT[n] == OWN else tok.at[PARENT[n]]).at[rows_of(i)], dst_ref=tok.at[n].at[rows_of(i)],
             send_sem=ag_send, recv_sem=ag_recv.at[n, i],
-            device_id=near(EDGES[n][1]), device_id_type=MESH,
+            device_id=near(TREE[n][1], TREE[n][2]), device_id_type=MESH,
         )
 
     def rs(n, i):
         return pltpu.make_async_remote_copy(
             src_ref=part.at[n].at[rows_of(i)], dst_ref=rsr.at[n].at[rows_of(i)],
             send_sem=rs_send, recv_sem=rs_recv.at[n, i],
-            device_id=near(EDGES[n][1] ^ 1), device_id_type=MESH,
+            device_id=near(TREE[n][1] ^ 1, TREE[n][2]), device_id_type=MESH,
         )
 
     def exchange(j):
@@ -140,59 +141,57 @@
             )
         ]
 
-    pl.semaphore_wait(bar, 4 + NPOP - 1)
-    for i in range(NCH):
-        for n in EDGE_GROUP[0]:
-            ag(n, i).start()
-
-    for s in range(SLOTS):
-        for n in GROUP[s]:
+    pl.semaphore_wait(bar, len(REACH) + NPOP - 1)
+
+    def load_weights():
+        for s in range(SLOTS):
+            for n in GROUP[s]:
+                cols = pl.ds(pl.multiple_of(source(n) * FB, FB), FB)
+                to = pl.ds(n * FB, FB)
+                pltpu.make_async_copy(wg_h.at[:, cols], wg.at[:, to], wsem.at[s]).start()
+                pltpu.make_async_copy(wu_h.at[:, cols], wu.at[:, to], wsem.at[8 + s]).start()
+        for s in reversed(range(SLOTS)):
+            for n in GROUP[s]:
+                cols = pl.ds(pl.multiple_of(source(n) * FB, FB), FB)
+                pltpu.make_async_copy(
+                    wd_h.at[:, cols], wd.at[pl.ds(0, FFB), pl.ds(n * FB, FB)], wsem.at[16 + s]
+                ).start()
+
+    def pack(h, s):
+        own.wait()
+
+        for c in small:
+            c.wait()
+        fsend[...] = jnp.zeros((8, 128), F32)
+        fsend[0:1, 0:8] = fit[...]
+        rf[...] = jnp.zeros((16, 512), F32)
+        for t, ref in enumerate((gr, ur, dl)):
+            for k in range(4):
+                rf[4 * k : 4 * k + 4, 0:FFB] = ref[k].astype(F32)
+            rsend[16 * t : 16 * t + 16, :] = rf[...].astype(BF)
+        for t, ref in enumerate((gl, ul, dr)):
+            for k in range(4):
+                lf[4 * k : 4 * k + 4, :] = ref[k].astype(F32)
+            lsend[16 * t : 16 * t + 16, :] = lf[...].astype(BF)
+        for j in range(1, NPOP):
+            for c in exchange(j):
+                c.start()
+        frecv[0] = fsend[...]
+        rrecv[0] = rsend[...]
+        lrecv[0] = lsend[:, pl.ds(pl.multiple_of(p * 512, 512), 512)]
+
+        zero16 = jnp.zeros((16, 512), BF)
+        rxg[...] = jnp.concatenate([rsend[0:16, :], rsend[0:16, :], zero16, zero16], axis=0)
+        rxu[...] = jnp.concatenate([zero16, zero16, rsend[16:32, :], rsend[16:32, :]], axis=0)
+        dlx[...] = jnp.concatenate([zero16] * 5 + [rsend[32:48, :], rsend[32:48, :], zero16], axis=0)
+        for n in range(32):
             cols = pl.ds(pl.multiple_of(source(n) * FB, FB), FB)
             to = pl.ds(n * FB, FB)
-            pltpu.make_async_copy(wg_h.at[:, cols], wg.at[:, to], wsem.at[s]).start()
-            pltpu.make_async_copy(wu_h.at[:, cols], wu.at[:, to], wsem.at[8 + s]).start()
-    for s in reversed(range(SLOTS)):
-        for n in GROUP[s]:
-            cols = pl.ds(pl.multiple_of(source(n) * FB, FB), FB)
-            pltpu.make_async_copy(
-                wd_h.at[:, cols], wd.at[pl.ds(0, FFB), pl.ds(n * FB, FB)], wsem.at[16 + s]
-            ).start()
-
-
-    own.wait()
-
-    for c in small:
-        c.wait()
-    fsend[...] = jnp.zeros((8, 128), F32)
-    fsend[0:1, 0:8] = fit[...]
-    rf[...] = jnp.zeros((16, 512), F32)
-    for t, ref in enumerate((gr, ur, dl)):
-        for k in range(4):
-            rf[4 * k : 4 * k + 4, 0:FFB] = ref[k].astype(F32)
-        rsend[16 * t : 16 * t + 16, :] = rf[...].astype(BF)
-    for t, ref in enumerate((gl, ul, dr)):
-        for k in range(4):
-            lf[4 * k : 4 * k + 4, :] = ref[k].astype(F32)
-        lsend[16 * t : 16 * t + 16, :] = lf[...].astype(BF)
-    for j in range(1, NPOP):
-        for c in exchange(j):
-            c.start()
-    frecv[0] = fsend[...]
-    rrecv[0] = rsend[...]
-    lrecv[0] = lsend[:, pl.ds(pl.multiple_of(p * 512, 512), 512)]
-
-    zero16 = jnp.zeros((16, 512), BF)
-    rxg[...] = jnp.concatenate([rsend[0:16, :], rsend[0:16, :], zero16, zero16], axis=0)
-    rxu[...] = jnp.concatenate([zero16, zero16, rsend[16:32, :], rsend[16:32, :]], axis=0)
-    dlx[...] = jnp.concatenate([zero16] * 5 + [rsend[32:48, :], rsend[32:48, :], zero16], axis=0)
-    for n in range(32):
-        cols = pl.ds(pl.multiple_of(source(n) * FB, FB), FB)
-        to = pl.ds(n * FB, FB)
-        a, b, c = lsend[0:16, cols], lsend[16:32, cols], lsend[32:48, cols]
-        lx[:, to] = jnp.concatenate([a, a, b, b], axis=0)
-        wd[FFB:512, to] = jnp.concatenate([c, c, jnp.zeros((16, FB), BF)], axis=0)
-        gainp[n : n + 1, :] = gain[pl.ds(source(n), 1), :]
-    hid[:, 384:512] = jnp.zeros((ROWS, 128), BF)
+            a, b, c = lsend[0:16, cols], lsend[16:32, cols], lsend[32:48, cols]
+            lx[:, to] = jnp.concatenate([a, a, b, b], axis=0)
+            wd[FFB:512, to] = jnp.concatenate([c, c, jnp.zeros((16, FB), BF)], axis=0)
+            gainp[n : n + 1, :] = gain[pl.ds(source(n), 1), :]
+        hid[:, 384:512] = jnp.zeros((ROWS, 128), BF)
 
     def project(s, h, first):
         rows = slice(h * HALF, h * HALF + HALF)
@@ -305,14 +304,13 @@
         seen.update((h, n) for n in new)
         return new
 
-    def send_slot(h, s):
-        wait = {n: arrive(h, [PARENT[n]]) for n in EDGE_GROUP[s]}
+    def send_on(h, n):
+        new = arrive(h, [PARENT[n]])
 
         def body(i):
-            for n in EDGE_GROUP[s]:
-                for q in wait[n]:
-                    ag(q, i).wait_recv()
-                ag(n, i).start()
+            for q in new:
+                ag(q, i).wait_recv()
+            ag(n, i).start()
 
         halves(h, body)
 
@@ -336,13 +334,12 @@
             wait_down(s)
         down(s, h)
 
-    def reduce_slot(h, s):
+    def send_back(h, n):
         def body(i):
-            for n in EDGE_GROUP[s]:
-                total = add_children(n, i)
-                if total is not None:
-                    part[n, rows_of(i), :] = total.astype(BF)
-                rs(n, i).start()
+            total = add_children(n, i)
+            if total is not None:
+                part[n, rows_of(i), :] = total.astype(BF)
+            rs(n, i).start()
 
         halves(h, body)
 
@@ -369,19 +366,21 @@
         outs[t].start()
 
     tasks = {
-        "S": send_slot, "P": project_slot, "F": finish, "D": down_slot,
-        "R": reduce_slot, "L": last, "X": weights_ready, "T": step_slot,
+        "S": send_on, "P": project_slot, "F": finish, "D": down_slot,
+        "R": send_back, "L": last, "X": weights_ready, "T": step_slot, "K": pack,
     }
-    for word in ORDER[2:]:
-        tasks[word[0]]("AB".index(word[1]), int(word[2]))
+    for at, word in enumerate(ORDER):
+        tasks[word[0]]("AB".index(word[1]), int(word[2:]))
+        if at == ROOTS:
+            load_weights()
 
     ag_all = pltpu.make_async_remote_copy(
         src_ref=tok.at[pl.ds(0, OWN)], dst_ref=tok.at[pl.ds(0, OWN)], send_sem=ag_send, recv_sem=ag_recv.at[0, 0],
-        device_id=near(0), device_id_type=MESH,
+        device_id=near(0, 1), device_id_type=MESH,
     )
     rs_all = pltpu.make_async_remote_copy(
         src_ref=part.at[pl.ds(0, OWN)], dst_ref=rsr, send_sem=rs_send, recv_sem=rs_recv.at[0, 0],
-        device_id=near(0), device_id_type=MESH,
+        device_id=near(0, 1), device_id_type=MESH,
     )
     ag_all.wait_send()
     rs_all.wait_send()
@@ -400,13 +399,13 @@
     mixed, gate_step, up_step, down_step = pl.pallas_call(
         kernel,
         out_shape=(
-            jax.ShapeDtypeStruct((ROWS, FB), BF),
-            jax.ShapeDtypeStruct((FFB, 512), BF),
-            jax.ShapeDtypeStruct((FFB, 512), BF),
-            jax.ShapeDtypeStruct((FFB, 512), BF),
+            pltpu.VMEM((ROWS, FB), BF),
+            pltpu.VMEM((FFB, 512), BF),
+            pltpu.VMEM((FFB, 512), BF),
+            pltpu.VMEM((FFB, 512), BF),
         ),
         in_specs=[anywhere] * 12,
-        out_specs=(pl.BlockSpec(memory_space=pltpu.VMEM), anywhere, anywhere, anywhere),
+        out_specs=(pl.BlockSpec(memory_space=pltpu.VMEM),) * 4,
         scratch_shapes=[
             vm((32, ROWS, FB), BF),
             vm((FFB, D), BF),
@@ -467,17 +466,15 @@
     return mixed, gate_step.T, up_step.T, down_step
 
 
-def move(a, b, c, d, a_out, b_out, c_out, d_out, a_mid, b_mid, c_mid, d_mid, sem):
-    steps = (((a, a_mid), (a_mid, a_out)), ((b, b_mid), (b_mid, b_out)), ((c, c_mid), (c_mid, c_out)), ((d, d_mid), (d_mid, d_out)))
-    first = [pltpu.make_async_copy(*one, sem.at[0, n]) for n, (one, _) in enumerate(steps)]
-    second = [pltpu.make_async_copy(*two, sem.at[1, n]) for n, (_, two) in enumerate(steps)]
-    for c in first:
+def move(a, b, c, d, a_out, b_out, c_out, d_out, sem):
+    copies = [
+        pltpu.make_async_copy(i, o, sem.at[n])
+        for n, (i, o) in enumerate(((b, b_out), (c, c_out), (d, d_out), (a, a_out)))
+    ]
+    for c in copies:
         c.start()
-    for c, d in zip(first, second):
+    for c in copies:
         c.wait()
-        d.start()
-    for d in second:
-        d.wait()
 
 
 def hand_over(*arrays):
@@ -487,7 +484,8 @@
         out_shape=tuple(jax.ShapeDtypeStruct(a.shape, a.dtype) for a in arrays),
         in_specs=[anywhere] * 4,
         out_specs=(anywhere,) * 4,
-        scratch_shapes=[pltpu.VMEM(a.shape, a.dtype) for a in arrays] + [pltpu.SemaphoreType.DMA((2, 4))],
+        scratch_shapes=[pltpu.SemaphoreType.DMA((4,))],
+        compiler_params=pltpu.CompilerParams(vmem_limit_bytes=1 << 20),
         name="hand_over",
     )(*arrays)
 

time: 66.5 us -> 65 us (0.977)
  Pallas kernels: 65.7 us -> 64.3 us
    pallas_call x1, Pallas kernels: 2.25 us -> 1.16 us  [hand_over(): pl.pallas_call(move, out_shape=tuple((jax.ShapeDtypeStruct(a.shape, a.dty...]
where the time goes in v4:
time: 65 us; the launch traced here: 64.9 us
  Pallas kernels  64.3 us (99%)
    pallas_call x1, Pallas kernels, per_device(): pl.pallas_call(kernel, out_shape=(pltpu.VMEM((ROWS, FB), BF), pltpu.VMEM(...  63.1 us

profile of v4, /device:TPU:8, one launch (start us, length us, event | category | flops | bytes accessed | tf_op | source)
XLA Modules:
  0.0 64.9 jit_solution(15003429699960090062)
XLA Ops:
  0.6 63.1 %es_step.1 = (bf16[512,128]{1,0:T(8,128)(2,1)S(1)}, bf16[464,512]{1,0:T(8,128)(2,1)S(1)}, bf16[464,512]{1,0:T(8,128)(2,1)S(1)}, bf16[464,512]{1,0:T(8,128)(2,1)S(1)}) custom-call(bf16[512,128]{1,0:T(8,128)(2,1)} %tok_h.1, f32[32,128]{1,0:T(8,128)} %bitcast.10, bf16[464,4096]{1,0:T(8,128)(2,1)} %bitcast.6, bf16[464,4096]{1,0:T(8,128)(2,1)} %bitcast.7, ...), custom_call_target="tpu_custom_call" | custom-call | flops 6499999744 | bytes 14000000 | tf_op jit(solution)/shard_map/es_step/pallas_call | solution.py:399
  63.7 1.2 %hand_over.1 = (bf16[512,128]{1,0:T(8,128)(2,1)}, bf16[464,512]{1,0:T(8,128)(2,1)}, bf16[464,512]{1,0:T(8,128)(2,1)}, bf16[464,512]{1,0:T(8,128)(2,1)}) custom-call(bf16[512,128]{1,0:T(8,128)(2,1)S(1)} %get-tuple-element.12.a, bf16[464,512]{1,0:T(8,128)(2,1)S(1)} %get-tuple-element.13.b, bf16[464,512]{1,0:T(8,128)(2,1)S(1)} %get-tuple-element.14.c, ...), custom_call_target="tpu_custom_call" | custom-call | tf_op jit(solution)/shard_map/hand_over/pallas_call | solution.py:482

commit v5 on v4

--- a/solution.py
+++ b/solution.py
@@ -18,38 +18,60 @@
 HALF = ROWS // 2
 SLOTS = 8
 
-TREE = (
-    ((1, 0), 0, 1, 31), ((3, 0), 1, 1, 31), ((0, 1), 2, 1, 31), ((0, 7), 3, 1, 31),
-    ((1, 1), 0, 1, 2), ((3, 7), 1, 1, 3), ((3, 1), 2, 1, 1), ((0, 6), 3, 1, 3),
-    ((1, 6), 0, 1, 7), ((2, 0), 1, 1, 1), ((0, 2), 2, 1, 2), ((0, 5), 3, 1, 7),
-    ((2, 1), 0, 1, 4), ((3, 6), 1, 1, 7), ((1, 2), 2, 1, 4), ((1, 7), 3, 1, 0),
-    ((2, 6), 0, 1, 8), ((2, 7), 1, 1, 5), ((0, 3), 2, 1, 10), ((1, 5), 3, 1, 8),
-    ((1, 3), 0, 1, 18), ((3, 5), 1, 1, 11), ((2, 2), 2, 1, 12), ((1, 4), 3, 1, 19),
-    ((2, 5), 0, 1, 19), ((3, 3), 1, 1, 18), ((3, 2), 2, 1, 6), ((0, 4), 3, 1, 11),
-    ((2, 3), 1, 1, 25), ((3, 4), 2, 1, 25), ((2, 4), 3, 1, 24),
+OFFSET = (
+    (3, 1), (3, 3), (2, 1), (0, 5), (2, 0), (3, 6), (3, 0), (1, 1), (3, 7), (1, 7), (1, 6), (0, 3),
+    (0, 6), (1, 0), (0, 1), (0, 2), (3, 5), (3, 2), (1, 4), (2, 6), (1, 2), (0, 7), (2, 7), (1, 5),
+    (0, 4), (1, 3), (2, 5), (2, 2), (3, 4), (2, 3), (2, 4),
+    (0, 0),
+)
+GATHER = (
+    (
+        (2, 1, 6), (1, 1, 11), (0, 1, 7), (3, 1, 12), (1, 1, 6), (1, 1, 12), (1, 1, 31), (0, 1, 14),
+        (1, 1, 21), (3, 1, 13), (0, 1, 12), (2, 1, 15), (3, 1, 21), (0, 1, 31), (2, 1, 31), (2, 1, 14),
+        (1, 1, 3), (1, 1, 15), (3, 1, 23), (0, 1, 10), (2, 1, 7), (3, 1, 31), (3, 1, 4), (3, 1, 10),
+        (3, 1, 3), (0, 1, 11), (0, 1, 23), (2, 1, 2), (2, 1, 1), (1, 1, 1), (3, 1, 26),
+    ),
+    (
+        (2, 1, 6), (1, 1, 11), (0, 1, 7), (3, 1, 12), (1, 1, 6), (1, 1, 12), (1, 1, 31), (0, 1, 14),
+        (1, 1, 21), (2, 1, 10), (0, 1, 12), (2, 1, 15), (3, 1, 21), (0, 1, 31), (2, 1, 31), (2, 1, 14),
+        (1, 1, 3), (1, 1, 15), (3, 1, 23), (0, 1, 10), (0, 1, 15), (3, 1, 31), (3, 1, 4), (3, 1, 10),
+        (2, 1, 11), (0, 1, 11), (0, 1, 23), (2, 1, 2), (2, 1, 1), (1, 1, 1), (3, 1, 26),
+    ),
+)
+SCATTER = (
+    (
+        (2, 1, 6), (1, 1, 11), (0, 1, 7), (3, 1, 12), (1, 1, 6), (1, 1, 12), (1, 1, 31), (0, 1, 14),
+        (1, 1, 21), (3, 1, 13), (0, 1, 12), (2, 1, 15), (3, 1, 21), (0, 1, 31), (2, 1, 31), (2, 1, 14),
+        (1, 1, 3), (2, 1, 0), (3, 1, 23), (0, 1, 10), (2, 1, 7), (3, 1, 31), (0, 1, 9), (3, 1, 10),
+        (3, 1, 3), (0, 1, 11), (0, 1, 23), (2, 1, 2), (2, 1, 1), (1, 1, 1), (3, 1, 26),
+    ),
+    (
+        (1, 1, 14), (1, 1, 11), (0, 1, 7), (3, 1, 12), (1, 1, 6), (1, 1, 12), (1, 1, 31), (0, 1, 14),
+        (1, 1, 21), (3, 1, 13), (0, 1, 12), (2, 1, 15), (3, 1, 21), (0, 1, 31), (2, 1, 31), (2, 1, 14),
+        (1, 1, 3), (2, 1, 0), (3, 1, 23), (0, 1, 10), (2, 1, 7), (3, 1, 31), (1, 1, 8), (3, 1, 10),
+        (3, 1, 3), (0, 1, 11), (0, 1, 23), (2, 1, 2), (2, 1, 1), (1, 1, 1), (3, 1, 26),
+    ),
 )
 OWN = 31
-OFFSET = [e[0] for e in TREE] + [(0, 0)]
-PARENT = [e[3] for e in TREE]
-CHILDREN = [[c for c in range(OWN) if PARENT[c] == n] for n in range(32)]
+CHILDREN = [[[c for c in range(OWN) if tree[c][2] == n] for n in range(32)] for tree in SCATTER]
 GROUP = [list(range(4 * s, 4 * s + 4)) for s in range(SLOTS)]
-REACH = sorted({(e[1], e[2]) for e in TREE} | {(e[1] ^ 1, e[2]) for e in TREE})
+REACH = sorted({(e[0] ^ turn, e[1]) for tree in GATHER + SCATTER for e in tree for turn in (0, 1)})
 
 ORDER = (
-    "SA3", "SA2", "SB3", "SA1", "SA0", "SB0", "SB1", "SB2", "KA0", "SA7", "SA10", "SA9", "SA4", "SB7",
-    "SB10", "SA5", "SB4", "SA15", "SA6", "SB5", "PB0", "SA8", "SA11", "SB9", "SA18", "SB8", "SB6", "SA13",
-    "SB11", "PA0", "SA12", "SB13", "SB18", "SA19", "SB12", "PA1", "SA14", "SB14", "SA25", "SB19", "SA20", "SA27",
-    "SB15", "SA17", "PA2", "SA26", "PB1", "SA24", "SA16", "SA23", "SB25", "PB2", "SA21", "SA22", "SA28", "SA29",
-    "SB24", "PA3", "SB16", "SB20", "SB26", "SA30", "SB27", "SB23", "SB17", "SB21", "PB3", "PA4", "SB28", "SB22",
-    "SB29", "XA0", "SB30", "PA6", "PA5", "PA7", "FA0", "DA7", "RA30", "DA5", "RA28", "RA21", "RA22", "RA20",
-    "RA29", "RA23", "DA6", "PB6", "RA27", "PB5", "DA4", "PB4", "RA16", "RA17", "RA26", "PB7", "FB0", "DB7",
-    "RB30", "RB28", "RB29", "DB6", "DB0", "DB5", "DB4", "RB22", "RA24", "DB3", "RB23", "DB1", "DA3", "RA25",
-    "RB26", "RB21", "RB20", "DA2", "RA11", "RA13", "RB14", "RA14", "RB27", "RB24", "DB2", "RB25", "DA0", "RB9",
-    "RB16", "RA19", "RA12", "RA18", "DA1", "RB12", "RA6", "RB19", "RA15", "TA0", "RB17", "RB11", "RB15", "RA9",
-    "RA8", "RB18", "RB6", "RB13", "RA5", "RB8", "RA4", "RB4", "RA10", "RB5", "RA7", "RB10", "RA1", "RB7",
-    "RB1", "RA0", "RA2", "RA3", "RB0", "RB2", "RB3", "TA1", "LA0", "TA2", "LB0",
+    "SA21", "SA14", "SB6", "SA6", "SA13", "SB14", "SB21", "SB13", "KA0", "SA12", "SA8", "SA15", "SA7", "SB4",
+    "SB12", "SB15", "SB7", "SA9", "SA4", "SB8", "SA10", "SA3", "SA11", "SB10", "SA5", "SA0", "SB3", "SB5",
+    "SB11", "SA2", "PB3", "SA20", "SA23", "SB2", "SB0", "SA1", "SA25", "SA17", "SB23", "PA3", "SA24", "PA2",
+    "SB9", "SA16", "SA22", "SA26", "SA27", "SA19", "SA18", "SB1", "PB1", "XA0", "SA28", "SA29", "SB26", "SB27",
+    "SB17", "PA1", "SB25", "SB16", "SA30", "SB19", "PA0", "SB24", "SB22", "PA5", "SB18", "PB2", "PA6", "SB20",
+    "SB29", "PB0", "SB30", "SB28", "PA4", "PA7", "FA0", "DA7", "RA30", "RA29", "DA6", "DA4", "DA1", "RA25",
+    "RA28", "RA16", "RA27", "RA17", "RA24", "RA18", "PB6", "RA4", "RA19", "PB4", "DA5", "PB5", "RA22", "PB7",
+    "FB0", "DB7", "RB30", "RB29", "RA26", "DB1", "DB5", "RB28", "DB4", "DB6", "RA5", "RB25", "RB27", "RB18",
+    "DB0", "DA0", "RA3", "RB17", "DA2", "RA1", "RB20", "DA3", "RB16", "RB26", "RA20", "RA23", "RB19", "RB1",
+    "RB24", "DB2", "RB5", "RB4", "RA2", "TA1", "RB2", "RA11", "RB23", "RA9", "RB22", "RA10", "DB3", "RB0",
+    "RA8", "RB11", "RB3", "RA0", "RB9", "RB10", "RA15", "RA7", "RA12", "RB7", "RB15", "RB8", "RB12", "RA13",
+    "RA6", "RB13", "RA14", "RA21", "RB6", "RB14", "RB21", "TA2", "TA0", "LA0", "LB0",
 )
-ROOTS = max(at for at in range(12) if ORDER[at][0] == "S" and PARENT[int(ORDER[at][2:])] == OWN)
+ROOTS = max(at for at in range(12) if ORDER[at][0] == "S" and GATHER["AB".index(ORDER[at][1])][int(ORDER[at][2:])][2] == OWN)
 
 
 def nt(a, b):
@@ -114,18 +136,20 @@
     def rows_of(i):
         return pl.ds(pl.multiple_of(i * RC, RC), RC)
 
-    def ag(n, i):
+    def ag(h, n, i):
+        k, hops, parent = GATHER[h][n]
         return pltpu.make_async_remote_copy(
-            src_ref=(tok_h if PARENT[n] == OWN else tok.at[PARENT[n]]).at[rows_of(i)], dst_ref=tok.at[n].at[rows_of(i)],
+            src_ref=(tok_h if parent == OWN else tok.at[parent]).at[rows_of(i)], dst_ref=tok.at[n].at[rows_of(i)],
             send_sem=ag_send, recv_sem=ag_recv.at[n, i],
-            device_id=near(TREE[n][1], TREE[n][2]), device_id_type=MESH,
+            device_id=near(k, hops), device_id_type=MESH,
         )
 
-    def rs(n, i):
+    def rs(h, n, i):
+        k, hops, _ = SCATTER[h][n]
         return pltpu.make_async_remote_copy(
             src_ref=part.at[n].at[rows_of(i)], dst_ref=rsr.at[n].at[rows_of(i)],
             send_sem=rs_send, recv_sem=rs_recv.at[n, i],
-            device_id=near(TREE[n][1] ^ 1, TREE[n][2]), device_id_type=MESH,
+            device_id=near(k ^ 1, hops), device_id_type=MESH,
         )
 
     def exchange(j):
@@ -248,12 +272,12 @@
         for q, n in enumerate(GROUP[s]):
             part[n, rows, :] = y[:, q * FB : (q + 1) * FB].astype(BF)
 
-    def add_children(n, i):
+    def add_children(h, n, i):
         rows = rows_of(i)
-        if CHILDREN[n]:
+        if CHILDREN[h][n]:
             total = part[n, rows, :].astype(F32)
-            for c in CHILDREN[n]:
-                rs(c, i).wait_recv()
+            for c in CHILDREN[h][n]:
+                rs(h, c, i).wait_recv()
                 total = total + rsr[c, rows, :].astype(F32)
             return total
         return None
@@ -274,15 +298,14 @@
         col = jnp.sum(wide * pick, axis=1, keepdims=True) * (1.0 / math.sqrt(128))
         wcol[...] = jnp.broadcast_to(col, (128, 128))
 
-    def step(t, i):
-        rows = rows_of(i)
+    def step(t):
         take = pl.ds(16 * t, 16)
-        left = rrecv[:, take, rows].reshape(128, 128).astype(F32).T.astype(BF)
-        right = lrecv[:, take, :].reshape(128, 512).astype(F32) * wcol[:, 0:1]
+        left = rrecv[:, take, :].reshape(128, 512).T
+        right = lrecv[:, take, :].reshape(128, 512).astype(F32) * jnp.concatenate([wcol[...]] * 4, axis=1)
         high = right.astype(BF)
         low = (right - high.astype(F32)).astype(BF)
         out = mm(jnp.concatenate([left, left], axis=1), jnp.concatenate([high, low], axis=0))
-        (gsb, usb, dsb)[t][rows, :] = out.astype(BF)
+        (gsb, usb, dsb)[t][...] = out.astype(BF)
 
     outs = [
         pltpu.make_async_copy(gsb.at[pl.ds(0, FFB)], gs_h, osem.at[0]),
@@ -305,12 +328,12 @@
         return new
 
     def send_on(h, n):
-        new = arrive(h, [PARENT[n]])
+        new = arrive(h, [GATHER[h][n][2]])
 
         def body(i):
             for q in new:
-                ag(q, i).wait_recv()
-            ag(n, i).start()
+                ag(h, q, i).wait_recv()
+            ag(h, n, i).start()
 
         halves(h, body)
 
@@ -323,7 +346,7 @@
 
         def body(i):
             for n in new:
-                ag(n, i).wait_recv()
+                ag(h, n, i).wait_recv()
 
         halves(h, body)
         project(s, h, first)
@@ -336,17 +359,17 @@
 
     def send_back(h, n):
         def body(i):
-            total = add_children(n, i)
+            total = add_children(h, n, i)
             if total is not None:
                 part[n, rows_of(i), :] = total.astype(BF)
-            rs(n, i).start()
+            rs(h, n, i).start()
 
         halves(h, body)
 
     def last(h, s):
         def body(i):
             rows = rows_of(i)
-            total = add_children(OWN, i) + tok[OWN, rows, :].astype(F32)
+            total = add_children(h, OWN, i) + tok[OWN, rows, :].astype(F32)
             mixed_ref[rows, :] = total.astype(BF)
 
         halves(h, body)
@@ -358,11 +381,7 @@
         shape_weights()
 
     def step_slot(h, t):
-        def run(i, carry):
-            step(t, i)
-            return carry
-
-        lax.fori_loop(0, NCH, run, 0)
+        step(t)
         outs[t].start()
 
     tasks = {

time: 65 us -> 63.6 us (0.978)
  Pallas kernels: 64.3 us -> 62.1 us
    pallas_call x1, Pallas kernels: 63.1 us -> 61 us  [per_device(): pl.pallas_call(kernel, out_shape=(pltpu.VMEM((ROWS, FB), BF), pltpu.VMEM(...]
where the time goes in v5:
time: 63.6 us; the launch traced here: 62.9 us
  Pallas kernels  62.1 us (98%)
  between operations  0.8 us (1%)
    pallas_call x1, Pallas kernels, per_device(): pl.pallas_call(kernel, out_shape=(pltpu.VMEM((ROWS, FB), BF), pltpu.VMEM(...  61 us

profile of v5, /device:TPU:8, one launch (start us, length us, event | category | flops | bytes accessed | tf_op | source)
XLA Modules:
  0.0 62.9 jit_solution(7529355993404525789)
XLA Ops:
  0.6 61.0 %es_step.1 = (bf16[512,128]{1,0:T(8,128)(2,1)S(1)}, bf16[464,512]{1,0:T(8,128)(2,1)S(1)}, bf16[464,512]{1,0:T(8,128)(2,1)S(1)}, bf16[464,512]{1,0:T(8,128)(2,1)S(1)}) custom-call(bf16[512,128]{1,0:T(8,128)(2,1)} %tok_h.1, f32[32,128]{1,0:T(8,128)} %bitcast.10, bf16[464,4096]{1,0:T(8,128)(2,1)} %bitcast.6, bf16[464,4096]{1,0:T(8,128)(2,1)} %bitcast.7, ...), custom_call_target="tpu_custom_call" | custom-call | flops 6499999744 | bytes 14000000 | tf_op jit(solution)/shard_map/es_step/pallas_call | solution.py:418
  61.6 1.2 %hand_over.1 = (bf16[512,128]{1,0:T(8,128)(2,1)}, bf16[464,512]{1,0:T(8,128)(2,1)}, bf16[464,512]{1,0:T(8,128)(2,1)}, bf16[464,512]{1,0:T(8,128)(2,1)}) custom-call(bf16[512,128]{1,0:T(8,128)(2,1)S(1)} %get-tuple-element.12.a, bf16[464,512]{1,0:T(8,128)(2,1)S(1)} %get-tuple-element.13.b, bf16[464,512]{1,0:T(8,128)(2,1)S(1)} %get-tuple-element.14.c, ...), custom_call_target="tpu_custom_call" | custom-call | tf_op jit(solution)/shard_map/hand_over/pallas_call | solution.py:501

commit v6 on v5

--- a/solution.py
+++ b/solution.py
@@ -19,37 +19,37 @@
 SLOTS = 8
 
 OFFSET = (
-    (3, 1), (3, 3), (2, 1), (0, 5), (2, 0), (3, 6), (3, 0), (1, 1), (3, 7), (1, 7), (1, 6), (0, 3),
-    (0, 6), (1, 0), (0, 1), (0, 2), (3, 5), (3, 2), (1, 4), (2, 6), (1, 2), (0, 7), (2, 7), (1, 5),
-    (0, 4), (1, 3), (2, 5), (2, 2), (3, 4), (2, 3), (2, 4),
+    (2, 1), (3, 1), (1, 2), (1, 0), (1, 1), (2, 0), (0, 1), (3, 6), (3, 5), (3, 0), (3, 3), (2, 7),
+    (0, 7), (3, 7), (0, 2), (0, 6), (1, 3), (0, 4), (2, 6), (1, 5), (1, 7), (0, 5), (0, 3), (1, 6),
+    (1, 4), (2, 5), (3, 2), (2, 2), (2, 3), (3, 4), (2, 4),
     (0, 0),
 )
 GATHER = (
     (
-        (2, 1, 6), (1, 1, 11), (0, 1, 7), (3, 1, 12), (1, 1, 6), (1, 1, 12), (1, 1, 31), (0, 1, 14),
-        (1, 1, 21), (3, 1, 13), (0, 1, 12), (2, 1, 15), (3, 1, 21), (0, 1, 31), (2, 1, 31), (2, 1, 14),
-        (1, 1, 3), (1, 1, 15), (3, 1, 23), (0, 1, 10), (2, 1, 7), (3, 1, 31), (3, 1, 4), (3, 1, 10),
-        (3, 1, 3), (0, 1, 11), (0, 1, 23), (2, 1, 2), (2, 1, 1), (1, 1, 1), (3, 1, 26),
+        (0, 1, 4), (2, 1, 9), (2, 1, 4), (0, 1, 31), (0, 1, 6), (1, 1, 9), (2, 1, 31), (1, 1, 15),
+        (1, 1, 21), (1, 1, 31), (1, 1, 22), (1, 1, 13), (3, 1, 31), (1, 1, 12), (2, 1, 6), (3, 1, 12),
+        (0, 1, 22), (3, 1, 21), (0, 1, 23), (3, 1, 23), (3, 1, 3), (3, 1, 15), (2, 1, 14), (0, 1, 15),
+        (3, 1, 19), (0, 1, 19), (2, 1, 1), (2, 1, 0), (1, 1, 10), (2, 1, 10), (3, 1, 25),
     ),
     (
-        (2, 1, 6), (1, 1, 11), (0, 1, 7), (3, 1, 12), (1, 1, 6), (1, 1, 12), (1, 1, 31), (0, 1, 14),
-        (1, 1, 21), (2, 1, 10), (0, 1, 12), (2, 1, 15), (3, 1, 21), (0, 1, 31), (2, 1, 31), (2, 1, 14),
-        (1, 1, 3), (1, 1, 15), (3, 1, 23), (0, 1, 10), (0, 1, 15), (3, 1, 31), (3, 1, 4), (3, 1, 10),
-        (2, 1, 11), (0, 1, 11), (0, 1, 23), (2, 1, 2), (2, 1, 1), (1, 1, 1), (3, 1, 26),
+        (0, 1, 4), (2, 1, 9), (2, 1, 4), (0, 1, 31), (0, 1, 6), (1, 1, 9), (2, 1, 31), (1, 1, 15),
+        (1, 1, 21), (1, 1, 31), (1, 1, 22), (0, 1, 20), (3, 1, 31), (1, 1, 12), (2, 1, 6), (3, 1, 12),
+        (0, 1, 22), (2, 1, 22), (1, 1, 7), (3, 1, 23), (3, 1, 3), (3, 1, 15), (2, 1, 14), (0, 1, 15),
+        (3, 1, 19), (0, 1, 19), (2, 1, 1), (0, 1, 2), (1, 1, 10), (2, 1, 10), (3, 1, 25),
     ),
 )
 SCATTER = (
     (
-        (2, 1, 6), (1, 1, 11), (0, 1, 7), (3, 1, 12), (1, 1, 6), (1, 1, 12), (1, 1, 31), (0, 1, 14),
-        (1, 1, 21), (3, 1, 13), (0, 1, 12), (2, 1, 15), (3, 1, 21), (0, 1, 31), (2, 1, 31), (2, 1, 14),
-        (1, 1, 3), (2, 1, 0), (3, 1, 23), (0, 1, 10), (2, 1, 7), (3, 1, 31), (0, 1, 9), (3, 1, 10),
-        (3, 1, 3), (0, 1, 11), (0, 1, 23), (2, 1, 2), (2, 1, 1), (1, 1, 1), (3, 1, 26),
+        (0, 1, 4), (2, 1, 9), (2, 1, 4), (0, 1, 31), (0, 1, 6), (1, 1, 9), (2, 1, 31), (1, 1, 15),
+        (1, 1, 21), (1, 1, 31), (1, 1, 22), (1, 1, 13), (3, 1, 31), (1, 1, 12), (2, 1, 6), (3, 1, 12),
+        (0, 1, 22), (2, 1, 22), (0, 1, 23), (3, 1, 23), (3, 1, 3), (3, 1, 15), (2, 1, 14), (0, 1, 15),
+        (3, 1, 19), (0, 1, 19), (2, 1, 1), (0, 1, 2), (1, 1, 10), (2, 1, 10), (3, 1, 25),
     ),
     (
-        (1, 1, 14), (1, 1, 11), (0, 1, 7), (3, 1, 12), (1, 1, 6), (1, 1, 12), (1, 1, 31), (0, 1, 14),
-        (1, 1, 21), (3, 1, 13), (0, 1, 12), (2, 1, 15), (3, 1, 21), (0, 1, 31), (2, 1, 31), (2, 1, 14),
-        (1, 1, 3), (2, 1, 0), (3, 1, 23), (0, 1, 10), (2, 1, 7), (3, 1, 31), (1, 1, 8), (3, 1, 10),
-        (3, 1, 3), (0, 1, 11), (0, 1, 23), (2, 1, 2), (2, 1, 1), (1, 1, 1), (3, 1, 26),
+        (0, 1, 4), (2, 1, 9), (2, 1, 4), (0, 1, 31), (0, 1, 6), (1, 1, 9), (2, 1, 31), (1, 1, 15),
+        (1, 1, 21), (1, 1, 31), (1, 1, 22), (1, 1, 13), (3, 1, 31), (1, 1, 12), (2, 1, 6), (3, 1, 12),
+        (0, 1, 22), (3, 1, 21), (0, 1, 23), (3, 1, 23), (3, 1, 3), (3, 1, 15), (2, 1, 14), (0, 1, 15),
+        (3, 1, 19), (0, 1, 19), (2, 1, 1), (2, 1, 0), (1, 1, 10), (2, 1, 10), (3, 1, 25),
     ),
 )
 OWN = 31
@@ -58,18 +58,18 @@
 REACH = sorted({(e[0] ^ turn, e[1]) for tree in GATHER + SCATTER for e in tree for turn in (0, 1)})
 
 ORDER = (
-    "SA21", "SA14", "SB6", "SA6", "SA13", "SB14", "SB21", "SB13", "KA0", "SA12", "SA8", "SA15", "SA7", "SB4",
-    "SB12", "SB15", "SB7", "SA9", "SA4", "SB8", "SA10", "SA3", "SA11", "SB10", "SA5", "SA0", "SB3", "SB5",
-    "SB11", "SA2", "PB3", "SA20", "SA23", "SB2", "SB0", "SA1", "SA25", "SA17", "SB23", "PA3", "SA24", "PA2",
-    "SB9", "SA16", "SA22", "SA26", "SA27", "SA19", "SA18", "SB1", "PB1", "XA0", "SA28", "SA29", "SB26", "SB27",
-    "SB17", "PA1", "SB25", "SB16", "SA30", "SB19", "PA0", "SB24", "SB22", "PA5", "SB18", "PB2", "PA6", "SB20",
-    "SB29", "PB0", "SB30", "SB28", "PA4", "PA7", "FA0", "DA7", "RA30", "RA29", "DA6", "DA4", "DA1", "RA25",
-    "RA28", "RA16", "RA27", "RA17", "RA24", "RA18", "PB6", "RA4", "RA19", "PB4", "DA5", "PB5", "RA22", "PB7",
-    "FB0", "DB7", "RB30", "RB29", "RA26", "DB1", "DB5", "RB28", "DB4", "DB6", "RA5", "RB25", "RB27", "RB18",
-    "DB0", "DA0", "RA3", "RB17", "DA2", "RA1", "RB20", "DA3", "RB16", "RB26", "RA20", "RA23", "RB19", "RB1",
-    "RB24", "DB2", "RB5", "RB4", "RA2", "TA1", "RB2", "RA11", "RB23", "RA9", "RB22", "RA10", "DB3", "RB0",
-    "RA8", "RB11", "RB3", "RA0", "RB9", "RB10", "RA15", "RA7", "RA12", "RB7", "RB15", "RB8", "RB12", "RA13",
-    "RA6", "RB13", "RA14", "RA21", "RB6", "RB14", "RB21", "TA2", "TA0", "LA0", "LB0",
+    "SA12", "SB12", "SA6", "SB9", "SA3", "SB6", "SB3", "SA9", "KA0", "SA15", "SA13", "SA14", "SA4", "SB5",
+    "SB15", "SB14", "SB4", "SA5", "SA1", "SA20", "SA23", "SA21", "SB13", "SA22", "SB23", "SB21", "SA7", "SB22",
+    "SA2", "SA0", "SB7", "SB2", "SB1", "SA19", "SB0", "PA3", "SB20", "SA10", "SA16", "SB19", "SA17", "SA8",
+    "SA26", "SA11", "SA25", "SA24", "PB1", "SA18", "SB10", "PB3", "SA27", "SA29", "PA1", "PA0", "SA28", "SB25",
+    "SB16", "SB18", "SA30", "SB26", "SB11", "PB5", "SB27", "SB17", "PA2", "SB24", "SB8", "PA4", "SB29", "PA5",
+    "PA6", "SB28", "SB30", "PB0", "PA7", "FA0", "DA4", "DA7", "RA17", "RA30", "RA16", "RA28", "DA2", "DA6",
+    "RA8", "RA27", "RA29", "RA24", "RA11", "RA26", "PB2", "PB4", "RA18", "PB6", "PB7", "FB0", "DB7", "RB30",
+    "RB29", "RB28", "DB4", "RA25", "DB6", "RB17", "DA3", "DA0", "RB27", "DA5", "RA10", "DB1", "RB16", "DB0",
+    "DB2", "RB24", "RA2", "RB8", "XA0", "RB26", "RB25", "RB18", "RA19", "RB10", "RB11", "RA0", "DB5", "RB2",
+    "RA21", "DA1", "RA1", "RA7", "DB3", "RB7", "RB0", "RB19", "RA22", "RA5", "RA23", "RB20", "TA2", "RB5",
+    "RB22", "RB21", "RA20", "RB1", "RB23", "RA13", "RA4", "RA14", "RA15", "RB4", "RB14", "RB13", "RB15", "RA9",
+    "RB9", "RA3", "RA6", "RA12", "RB3", "RB6", "RB12", "TA1", "TA0", "LA0", "LB0",
 )
 ROOTS = max(at for at in range(12) if ORDER[at][0] == "S" and GATHER["AB".index(ORDER[at][1])][int(ORDER[at][2:])][2] == OWN)
 

time: 63.6 us -> 64.4 us (1.013)
  Pallas kernels: 62.1 us -> 63.6 us
    pallas_call x1, Pallas kernels: 61 us -> 62.4 us  [per_device(): pl.pallas_call(kernel, out_shape=(pltpu.VMEM((ROWS, FB), BF), pltpu.VMEM(...]
where the time goes in v6:
time: 64.4 us
  Pallas kernels  63.6 us (99%)
  between operations  0.8 us (1%)
    pallas_call x1, Pallas kernels, per_device(): pl.pallas_call(kernel, out_shape=(pltpu.VMEM((ROWS, FB), BF), pltpu.VMEM(...  62.4 us

profile of v6, /device:TPU:8, one launch (start us, length us, event | category | flops | bytes accessed | tf_op | source)
XLA Modules:
  0.0 64.4 jit_solution(17155375875038386063)
XLA Ops:
  0.6 62.4 %es_step.1 = (bf16[512,128]{1,0:T(8,128)(2,1)S(1)}, bf16[464,512]{1,0:T(8,128)(2,1)S(1)}, bf16[464,512]{1,0:T(8,128)(2,1)S(1)}, bf16[464,512]{1,0:T(8,128)(2,1)S(1)}) custom-call(bf16[512,128]{1,0:T(8,128)(2,1)} %tok_h.1, f32[32,128]{1,0:T(8,128)} %bitcast.10, bf16[464,4096]{1,0:T(8,128)(2,1)} %bitcast.6, bf16[464,4096]{1,0:T(8,128)(2,1)} %bitcast.7, ...), custom_call_target="tpu_custom_call" | custom-call | flops 6499999744 | bytes 14000000 | tf_op jit(solution)/shard_map/es_step/pallas_call | solution.py:418
  63.0 1.2 %hand_over.1 = (bf16[512,128]{1,0:T(8,128)(2,1)}, bf16[464,512]{1,0:T(8,128)(2,1)}, bf16[464,512]{1,0:T(8,128)(2,1)}, bf16[464,512]{1,0:T(8,128)(2,1)}) custom-call(bf16[512,128]{1,0:T(8,128)(2,1)S(1)} %get-tuple-element.12.a, bf16[464,512]{1,0:T(8,128)(2,1)S(1)} %get-tuple-element.13.b, bf16[464,512]{1,0:T(8,128)(2,1)S(1)} %get-tuple-element.14.c, ...), custom_call_target="tpu_custom_call" | custom-call | tf_op jit(solution)/shard_map/hand_over/pallas_call | solution.py:501
